TPU v7x, 32 devices: a whole 2x2x4 slice. The times are simulated.
32 devices in a mesh: gx: 8 (over y, x, core), gy: 4 (over z).
Axes of the slice: x: 2, y: 2, z: 4, core: 2. Of those that a mesh axis runs over, the one named last changes fastest.
Arguments:
- tokens: bfloat16 [2, 16, 32, 32, 512], P(None, None, 'gx', 'gy'), may hold values from -6 to 6
- norm_gain: float32 [512], replicated, may hold values from 0.1 to 1.9
- w_qkv: bfloat16 [512, 1536], replicated, may hold values from -12 to 12
- w_out: bfloat16 [512, 512], replicated, may hold values from -1 to 1
Outputs:
- result: bfloat16 [2, 16, 32, 32, 512], P(None, None, 'gx', 'gy')
All inputs are finite; a program needn't handle non-finite values.
Results may differ from a plain program's by a relative error of at most 0.0095.
Values may be sent and summed in bfloat16 or wider, within the bound.
No kernel may reach another device: no remote copies, remote signals or barrier semaphores. Data moves between devices by JAX's collectives and lax.ppermute only.
A program may use at most 64 MiB of HBM per device.

v0:
```python
import jax
import jax.numpy as jnp
from jax import lax
from jax.sharding import PartitionSpec as P

HEADS = 8


def attend(triple, seq_dim):
    shape = triple.shape
    width = shape[-1] // 3
    head_size = width // HEADS
    split = shape[:-1] + (HEADS, head_size)
    queries = triple[..., :width].reshape(split)
    key_part = triple[..., width : 2 * width].reshape(split)
    values = triple[..., 2 * width :].reshape(split)
    if seq_dim == 1:
        form_scores, form_mix = ("asche,atche->achst", "achst,atche->asche")
    else:
        form_scores, form_mix = ("acshe,acthe->achst", "achst,acthe->acshe")
    scores = jnp.einsum(
        form_scores, queries, key_part, preferred_element_type=jnp.float32
    ) / jnp.sqrt(jnp.float32(head_size))
    highest = jnp.max(scores, axis=-1, keepdims=True)
    expo = jnp.exp(scores - highest)
    weights = (expo / jnp.sum(expo, axis=-1, keepdims=True)).astype(jnp.bfloat16)
    mixed = jnp.einsum(form_mix, weights, values, preferred_element_type=jnp.float32)
    return mixed.reshape(shape[:-1] + (width,)).astype(jnp.bfloat16)


def project(normed, w_qkv):
    width = normed.shape[-1]
    flat = jnp.dot(normed.reshape(-1, width), w_qkv, preferred_element_type=jnp.float32).astype(
        jnp.bfloat16
    )
    return flat.reshape(normed.shape[:-1] + (3 * width,))


def body(tokens, norm_gain, w_qkv, w_out):
    batch, steps, cells_x, cells_y, width = tokens.shape
    field = tokens.astype(jnp.float32)
    normed = (
        field * lax.rsqrt(jnp.mean(field * field, axis=-1, keepdims=True) + 1e-05) * norm_gain
    ).astype(jnp.bfloat16)
    triple = project(normed, w_qkv)
    along_time = attend(triple.reshape(batch, steps, cells_x * cells_y, 3 * width), 1)
    along_time = along_time.reshape(batch, steps, cells_x, cells_y, width)
    line_rows = batch * steps
    outgoing = normed.reshape(line_rows, cells_x, cells_y, width)

    def prepared(incoming):
        return project(incoming, w_qkv)

    outcome = attend(
        prepared(lax.all_to_all(outgoing, "gx", split_axis=0, concat_axis=1, tiled=True)), 1
    )
    along_x = lax.all_to_all(outcome, "gx", split_axis=1, concat_axis=0, tiled=True)
    outcome = attend(
        prepared(lax.all_to_all(outgoing, "gy", split_axis=0, concat_axis=2, tiled=True)), 2
    )
    along_y = lax.all_to_all(outcome, "gy", split_axis=2, concat_axis=0, tiled=True)
    mixed = (
        along_time.astype(jnp.float32)
        + along_x.reshape(along_time.shape).astype(jnp.float32)
        + along_y.reshape(along_time.shape).astype(jnp.float32)
    ).astype(jnp.bfloat16)
    update = jnp.dot(mixed.reshape(-1, width), w_out, preferred_element_type=jnp.float32)
    return (field + update.reshape(field.shape)).astype(jnp.bfloat16)


def solution(mesh):
    placed = (P(None, None, "gx", "gy", None), P(), P(), P())
    return jax.shard_map(
        body, mesh=mesh, in_specs=placed, out_specs=P(None, None, "gx", "gy", None), check_vma=False
    )
```

profile of v0, /device:TPU:0, one launch (start us, length us, event | category | flops | bytes accessed | tf_op | source)
XLA Modules:
  0.0 142.6 jit_solution(7588632968217393622)
XLA Ops:
  0.0 0.0 copy-start
  0.0 1.6 %fusion.12 = f32[2,16,4,8]{3,2,1,0:T(4,128)S(1)} fusion(bf16[2,16,4,8,512]{4,3,2,1,0:T(8,128)(2,1)} %param.4), kind=kLoop, calls=%fused_computation.22 | loop fusion | flops 1571840 | bytes 1052672 | tf_op jit(solution)/shard_map/reduce_sum | solution.py:43
  1.7 2.5 %fusion.14 = bf16[2,16,4,8,512]{4,3,2,1,0:T(8,128)(2,1)} fusion(bf16[2,16,4,8,512]{4,3,2,1,0:T(8,128)(2,1)} %param.4, f32[512]{0:T(512)} %param.5, f32[2,16,4,8]{3,2,1,0:T(4,128)S(1)} %add_rsqrt_fusion), kind=kLoop, calls=%fused_computation.24 | loop fusion | flops 2097152 | bytes 2103296 | tf_op jit(solution)/shard_map/convert_element_type | solution.py:44
  4.2 5.2 %all-to-all-start = ((bf16[32,4,8,512]{3,2,1,0:T(8,128)(2,1)}), bf16[32,4,8,512]{3,2,1,0:T(8,128)(2,1)}, u32[]{:S(2)}, u32[]{:S(2)}) async-start(bf16[32,4,8,512]{3,2,1,0:T(8,128)(2,1)} %bitcast.3), calls=%async_computation | async-start | bytes 2097152 | tf_op jit(solution)/shard_map/all_to_all | solution.py:55
  9.4 0.0 copy-done
  9.4 3.0 %convolution_convert_fusion.2 = bf16[1024,1536]{1,0:T(8,128)(2,1)S(1)} fusion(bf16[1024,512]{1,0:T(8,128)(2,1)} %bitcast, bf16[512,1536]{1,0:T(8,128)(2,1)S(1)} %copy-done), kind=kOutput, calls=%fused_computation.12 | convolution fusion | flops 1612185600 | bytes 5767168 | tf_op jit(solution)/shard_map/dot_general | solution.py:33
  12.4 1.7 %fusion.50 = (bf16[2,16,32,512]{3,2,1,0:T(8,128)(2,1)S(1)}, bf16[2,16,32,512]{3,2,1,0:T(8,128)(2,1)}, bf16[2,16,32,512]{3,2,1,0:T(8,128)(2,1)}) fusion(bf16[2,16,32,1536]{3,2,1,0:T(8,128)(2,1)S(1)} %bitcast.86), kind=kLoop, calls=%fused_computation.60 | loop fusion | bytes 6291456 | tf_op jit(solution)/shard_map/slice | solution.py:16
  14.1 3.9 %reshape.96 = bf16[2,16,32,8,64]{4,3,2,1,0:T(8,128)(2,1)} reshape(bf16[2,16,32,512]{3,2,1,0:T(8,128)(2,1)} %get-tuple-element.9) | data formatting | bytes 2097152 | tf_op jit(solution)/shard_map/reshape | solution.py:15
  18.0 3.9 %reshape.95 = bf16[2,16,32,8,64]{4,3,2,1,0:T(8,128)(2,1)} reshape(bf16[2,16,32,512]{3,2,1,0:T(8,128)(2,1)} %get-tuple-element.10) | data formatting | bytes 2097152 | tf_op jit(solution)/shard_map/reshape | solution.py:14
  21.9 3.0 %all-to-all-done = bf16[32,4,8,512]{3,2,1,0:T(8,128)(2,1)} async-done(((bf16[32,4,8,512]{3,2,1,0:T(8,128)(2,1)}), bf16[32,4,8,512]{3,2,1,0:T(8,128)(2,1)}, u32[]{:S(2)}, u32[]{:S(2)}) %all-to-all-start) | async-done | bytes 1048608 | tf_op jit(solution)/shard_map/all_to_all | solution.py:55
  24.9 5.3 %all-to-all-start.2 = ((bf16[32,4,8,512]{3,2,1,0:T(8,128)(2,1)}), bf16[32,4,8,512]{3,2,1,0:T(8,128)(2,1)}, u32[]{:S(2)}, u32[]{:S(2)}) async-start(bf16[32,4,8,512]{3,2,1,0:T(8,128)(2,1)} %bitcast.3), calls=%async_computation.2 | async-start | bytes 2097152 | tf_op jit(solution)/shard_map/all_to_all | solution.py:59
  30.2 1.3 copy.49
  31.5 1.8 %convolution_convert_fusion.1 = bf16[1024,1536]{1,0:T(8,128)(2,1)S(1)} fusion(bf16[1024,512]{1,0:T(8,128)(2,1)S(1)} %bitcast.87, bf16[512,1536]{1,0:T(8,128)(2,1)S(1)} %copy-done), kind=kOutput, calls=%fused_computation.11 | convolution fusion | flops 1612185600 | bytes 5767168 | tf_op jit(solution)/shard_map/dot_general | solution.py:33
  33.3 1.8 %fusion.49 = (bf16[4,32,8,512]{3,2,1,0:T(8,128)(2,1)}, bf16[4,32,8,512]{3,2,1,0:T(8,128)(2,1)}, bf16[4,32,8,512]{3,2,1,0:T(8,128)(2,1)}) fusion(bf16[4,32,8,1536]{3,2,1,0:T(8,128)(2,1)S(1)} %bitcast.84), kind=kLoop, calls=%fused_computation.59 | loop fusion | bytes 6291456 | tf_op jit(solution)/shard_map/slice | solution.py:16
  35.1 3.9 %reshape.102 = bf16[4,32,8,8,64]{4,3,2,1,0:T(8,128)(2,1)} reshape(bf16[4,32,8,512]{3,2,1,0:T(8,128)(2,1)} %get-tuple-element.6) | data formatting | bytes 2097152 | tf_op jit(solution)/shard_map/reshape | solution.py:15
  39.0 3.9 %reshape.101 = bf16[4,32,8,8,64]{4,3,2,1,0:T(8,128)(2,1)} reshape(bf16[4,32,8,512]{3,2,1,0:T(8,128)(2,1)} %get-tuple-element.7) | data formatting | bytes 2097152 | tf_op jit(solution)/shard_map/reshape | solution.py:14
  42.9 3.9 %reshape.100 = bf16[4,32,8,8,64]{4,3,2,1,0:T(8,128)(2,1)} reshape(bf16[4,32,8,512]{3,2,1,0:T(8,128)(2,1)} %get-tuple-element.5) | data formatting | bytes 2097152 | tf_op jit(solution)/shard_map/reshape | solution.py:16
  46.8 4.9 %fusion.25 = f32[4,8,8,32,32]{3,4,2,1,0:T(8,128)S(1)} fusion(bf16[4,32,8,8,64]{4,3,2,1,0:T(8,128)(2,1)} %reshape.102, bf16[4,32,8,8,64]{4,3,2,1,0:T(8,128)(2,1)} %reshape.101), kind=kOutput, calls=%fused_computation.39 | convolution fusion | flops 33554432 | bytes 3145728 | tf_op jit(solution)/shard_map/asche,atche->achst/dot_general | solution.py:21
  51.7 0.0 copy-start.5
  51.7 10.3 %fusion.54 = (f32[4,8,8,32]{3,2,1,0:T(8,128)S(1)}, f32[4,8,8,32,32]{3,4,2,1,0:T(8,128)S(1)}) fusion(f32[4,8,8,32,32]{3,4,2,1,0:T(8,128)S(1)} %fusion.25), kind=kOutput, calls=%fused_computation.64 | output fusion | flops 1048607 | bytes 2129920 | tf_op jit(solution)/shard_map/sub | solution.py:25
  62.0 0.0 copy-done.5
  62.0 1.8 %convert_bitcast_fusion.4 = bf16[4,32,8,8,64]{4,1,3,2,0:T(8,128)(2,1)S(1)} fusion(f32[4,8,8,32,32]{3,4,2,1,0:T(8,128)S(1)} %get-tuple-element.19, f32[4,8,8,32]{3,2,1,0:T(8,128)S(1)} %get-tuple-element.18, bf16[4,32,8,8,64]{4,3,2,1,0:T(8,128)(2,1)S(1)} %copy-done.5), kind=kOutput, calls=%fused_computation.49 | convolution fusion | flops 34603008 | bytes 3178496 | tf_op jit(solution)/shard_map/achst,atche->asche/dot_general | solution.py:27
  63.8 2.2 %copy.71 = bf16[4,32,8,8,64]{4,3,2,0,1:T(8,128)(2,1)} copy(bf16[4,32,8,8,64]{4,1,3,2,0:T(8,128)(2,1)S(1)} %convert_bitcast_fusion.4) | data formatting | bytes 2097152 | tf_op jit(solution)/shard_map/convert_element_type | solution.py:28
  66.0 4.0 %reshape.114 = bf16[4,32,8,512]{3,2,0,1:T(8,128)(2,1)} reshape(bf16[4,32,8,8,64]{4,3,2,0,1:T(8,128)(2,1)} %copy.71) | data formatting | bytes 2097152 | tf_op jit(solution)/shard_map/convert_element_type | solution.py:28
  70.1 0.0 all-to-all-done.2
  70.1 4.5 %all-to-all-start.1 = ((bf16[4,32,8,512]{3,2,0,1:T(8,128)(2,1)}), bf16[4,32,8,512]{3,2,0,1:T(8,128)(2,1)}, u32[]{:S(2)}, u32[]{:S(2)}) async-start(bf16[4,32,8,512]{3,2,0,1:T(8,128)(2,1)} %reshape.114), calls=%async_computation.1 | async-start | bytes 2097152 | tf_op jit(solution)/shard_map/all_to_all | solution.py:57
  74.5 1.3 copy.58
  75.9 1.8 %convolution_convert_fusion = bf16[1024,1536]{1,0:T(8,128)(2,1)S(1)} fusion(bf16[1024,512]{1,0:T(8,128)(2,1)S(1)} %bitcast.88, bf16[512,1536]{1,0:T(8,128)(2,1)S(1)} %copy-done), kind=kOutput, calls=%fused_computation.10 | convolution fusion | flops 1612185600 | bytes 5767168 | tf_op jit(solution)/shard_map/dot_general | solution.py:33
  77.7 1.7 %fusion.51 = (bf16[8,4,32,512]{3,2,1,0:T(8,128)(2,1)S(1)}, bf16[8,4,32,512]{3,2,1,0:T(8,128)(2,1)}, bf16[8,4,32,512]{3,2,1,0:T(8,128)(2,1)}) fusion(bf16[8,4,32,1536]{3,2,1,0:T(8,128)(2,1)S(1)} %bitcast.85), kind=kLoop, calls=%fused_computation.61 | loop fusion | bytes 6291456 | tf_op jit(solution)/shard_map/slice | solution.py:16
  79.3 3.9 %reshape.107 = bf16[8,4,32,8,64]{4,3,2,1,0:T(8,128)(2,1)} reshape(bf16[8,4,32,512]{3,2,1,0:T(8,128)(2,1)} %get-tuple-element.12) | data formatting | bytes 2097152 | tf_op jit(solution)/shard_map/reshape | solution.py:15
  83.2 3.9 %reshape.106 = bf16[8,4,32,8,64]{4,3,2,1,0:T(8,128)(2,1)} reshape(bf16[8,4,32,512]{3,2,1,0:T(8,128)(2,1)} %get-tuple-element.13) | data formatting | bytes 2097152 | tf_op jit(solution)/shard_map/reshape | solution.py:14
  87.1 3.4 %fusion.21 = f32[8,4,8,32,32]{3,4,2,1,0:T(8,128)S(1)} fusion(bf16[8,4,32,8,64]{4,3,2,1,0:T(8,128)(2,1)} %reshape.107, bf16[8,4,32,8,64]{4,3,2,1,0:T(8,128)(2,1)} %reshape.106), kind=kOutput, calls=%fused_computation.35 | convolution fusion | flops 33554432 | bytes 3145728 | tf_op jit(solution)/shard_map/acshe,acthe->achst/dot_general | solution.py:21
  90.6 3.2 %fusion.52 = (f32[8,4,8,32]{3,2,1,0:T(8,128)S(1)}, f32[8,4,8,32,32]{3,4,2,1,0:T(8,128)}) fusion(f32[8,4,8,32,32]{3,4,2,1,0:T(8,128)S(1)} %fusion.21), kind=kOutput, calls=%fused_computation.62 | output fusion | flops 1048607 | bytes 2129920 | tf_op jit(solution)/shard_map/sub | solution.py:25
  93.8 2.0 %reshape.105 = bf16[8,4,32,8,64]{4,3,2,1,0:T(8,128)(2,1)} reshape(bf16[8,4,32,512]{3,2,1,0:T(8,128)(2,1)S(1)} %get-tuple-element.11) | data formatting | bytes 2097152 | tf_op jit(solution)/shard_map/reshape | solution.py:16
  95.8 3.7 %convert_bitcast_fusion.3 = bf16[8,4,32,8,64]{4,2,3,1,0:T(8,128)(2,1)S(1)} fusion(f32[8,4,8,32,32]{3,4,2,1,0:T(8,128)} %get-tuple-element.15, f32[8,4,8,32]{3,2,1,0:T(8,128)S(1)} %get-tuple-element.14, bf16[8,4,32,8,64]{4,3,2,1,0:T(8,128)(2,1)} %reshape.105), kind=kOutput, calls=%fused_computation.46 | convolution fusion | flops 34603008 | bytes 3178496 | tf_op jit(solution)/shard_map/achst,acthe->acshe/dot_general | solution.py:27
  99.6 2.2 %copy.72 = bf16[8,4,32,8,64]{4,3,1,0,2:T(8,128)(2,1)} copy(bf16[8,4,32,8,64]{4,2,3,1,0:T(8,128)(2,1)S(1)} %convert_bitcast_fusion.3) | data formatting | bytes 2097152 | tf_op jit(solution)/shard_map/convert_element_type | solution.py:28
  101.7 4.2 %reshape.115 = bf16[8,4,32,512]{3,1,0,2:T(4,128)(2,1)} reshape(bf16[8,4,32,8,64]{4,3,1,0,2:T(8,128)(2,1)} %copy.72) | data formatting | bytes 2097152 | tf_op jit(solution)/shard_map/convert_element_type | solution.py:28
  105.9 0.0 all-to-all-done.1
  105.9 5.1 %all-to-all-start.3 = ((bf16[8,4,32,512]{3,1,0,2:T(4,128)(2,1)}), bf16[8,4,32,512]{3,1,0,2:T(4,128)(2,1)S(1)}, u32[]{:S(2)}, u32[]{:S(2)}) async-start(bf16[8,4,32,512]{3,1,0,2:T(4,128)(2,1)} %reshape.115), calls=%async_computation.3 | async-start | bytes 2097152 | tf_op jit(solution)/shard_map/all_to_all | solution.py:61
  111.0 6.7 %fusion.29 = f32[2,32,8,16,16]{3,4,2,1,0:T(8,128)} fusion(bf16[2,16,32,8,64]{4,3,2,1,0:T(8,128)(2,1)} %reshape.96, bf16[2,16,32,8,64]{4,3,2,1,0:T(8,128)(2,1)} %reshape.95), kind=kOutput, calls=%fused_computation.43 | convolution fusion | flops 16777216 | bytes 2621440 | tf_op jit(solution)/shard_map/asche,atche->achst/dot_general | solution.py:21
  117.7 2.1 %reshape.94 = bf16[2,16,32,8,64]{4,3,2,1,0:T(8,128)(2,1)} reshape(bf16[2,16,32,512]{3,2,1,0:T(8,128)(2,1)S(1)} %get-tuple-element.8) | data formatting | bytes 2097152 | tf_op jit(solution)/shard_map/reshape | solution.py:16
  119.8 0.0 copy-start.6
  119.8 5.5 %fusion.53 = (f32[2,32,8,16]{3,2,1,0:T(8,128)S(1)}, f32[2,32,8,16,16]{3,4,2,1,0:T(8,128)S(1)}) fusion(f32[2,32,8,16,16]{3,4,2,1,0:T(8,128)} %fusion.29), kind=kOutput, calls=%fused_computation.63 | output fusion | flops 524303 | bytes 1081344 | tf_op jit(solution)/shard_map/sub | solution.py:25
  125.3 0.0 copy-done.6
  125.3 1.7 %convert_bitcast_fusion = f32[2,16,32,8,64]{4,1,3,2,0:T(8,128)S(1)} fusion(f32[2,32,8,16,16]{3,4,2,1,0:T(8,128)S(1)} %get-tuple-element.17, f32[2,32,8,16]{3,2,1,0:T(8,128)S(1)} %get-tuple-element.16, bf16[2,16,32,8,64]{4,3,2,1,0:T(8,128)(2,1)S(1)} %copy-done.6), kind=kOutput, calls=%fused_computation.3 | convolution fusion | flops 18087936 | bytes 3702784 | tf_op jit(solution)/shard_map/achst,atche->asche/dot_general | solution.py:27
  127.0 3.2 %copy.48 = f32[2,16,32,8,64]{4,3,2,1,0:T(8,128)} copy(f32[2,16,32,8,64]{4,1,3,2,0:T(8,128)S(1)} %convert_bitcast_fusion) | data formatting | bytes 4194304 | tf_op jit(solution)/shard_map/convert_element_type | solution.py:63
  130.2 4.8 %reshape.108 = f32[2,16,4,8,512]{4,3,2,1,0:T(8,128)} reshape(f32[2,16,32,8,64]{4,3,2,1,0:T(8,128)} %copy.48) | data formatting | bytes 4194304 | tf_op jit(solution)/shard_map/convert_element_type | solution.py:63
  135.0 1.3 copy.56
  136.3 0.3 convert_bitcast_fusion.2
  136.6 1.5 %copy.57 = f32[8,4,4,8,512]{4,3,2,1,0:T(8,128)} copy(f32[8,4,4,8,512]{4,3,2,0,1:T(8,128)S(1)} %convert_bitcast_fusion.2) | data formatting | bytes 4194304 | tf_op jit(solution)/shard_map/convert_element_type | solution.py:64
  138.1 0.0 all-to-all-done.3
  138.1 0.0 copy-start.4
  138.1 0.6 convert_bitcast_fusion.1
  138.7 0.0 copy-start.2
  138.8 0.0 copy-start.3
  138.8 0.0 copy-start.7
  138.8 0.2 copy.66
  139.0 0.8 copy-done.4
  139.7 0.4 copy-done.2
  140.1 0.7 copy-done.3
  140.8 0.1 copy-done.7
  140.9 0.0 copy-start.1
  140.9 1.7 %fusion.15 = bf16[2,16,4,8,512]{4,3,2,1,0:T(8,128)(2,1)} fusion(bf16[2,16,4,8,512]{4,3,2,1,0:T(8,128)(2,1)S(1)} %copy-done.2, f32[2,16,4,8,512]{4,3,2,1,0:T(8,128)S(1)} %copy-done.3, bf16[512,512]{1,0:T(8,128)(2,1)S(1)} %copy-done.7, f32[2,16,4,8,512]{4,3,2,1,0:T(8,128)S(1)} %bitcast.82, f32[2,16,4,8,512]{4,3,2,1,0:T(8,128)S(1)} %bitcast.81), kind=kOutput, calls=%fused_computation.25 | convolution fusion | flops 540016640 | bytes 8912896 | tf_op jit(solution)/shard_map/dot_general | solution.py:67
  142.6 0.0 copy-done.1
  (1 shorter events, 0.0 us)
Async XLA Ops:
  0.0 9.4 %copy-start = (bf16[512,1536]{1,0:T(8,128)(2,1)S(1)}, bf16[512,1536]{1,0:T(8,128)(2,1)}, u32[]{:S(2)}) copy-start(bf16[512,1536]{1,0:T(8,128)(2,1)} %param.6) | copy-start | bytes 4718596
  4.2 20.7 %all-to-all-start = ((bf16[32,4,8,512]{3,2,1,0:T(8,128)(2,1)}), bf16[32,4,8,512]{3,2,1,0:T(8,128)(2,1)}, u32[]{:S(2)}, u32[]{:S(2)}) async-start(bf16[32,4,8,512]{3,2,1,0:T(8,128)(2,1)} %bitcast.3), calls=%async_computation | async-start | bytes 2097152 | tf_op jit(solution)/shard_map/all_to_all | solution.py:55
  24.9 45.2 %all-to-all-start.2 = ((bf16[32,4,8,512]{3,2,1,0:T(8,128)(2,1)}), bf16[32,4,8,512]{3,2,1,0:T(8,128)(2,1)}, u32[]{:S(2)}, u32[]{:S(2)}) async-start(bf16[32,4,8,512]{3,2,1,0:T(8,128)(2,1)} %bitcast.3), calls=%async_computation.2 | async-start | bytes 2097152 | tf_op jit(solution)/shard_map/all_to_all | solution.py:59
  51.7 10.3 %copy-start.5 = (bf16[4,32,8,8,64]{4,3,2,1,0:T(8,128)(2,1)S(1)}, bf16[4,32,8,8,64]{4,3,2,1,0:T(8,128)(2,1)}, u32[]{:S(2)}) copy-start(bf16[4,32,8,8,64]{4,3,2,1,0:T(8,128)(2,1)} %reshape.100) | copy-start | bytes 3145732
  70.1 35.9 %all-to-all-start.1 = ((bf16[4,32,8,512]{3,2,0,1:T(8,128)(2,1)}), bf16[4,32,8,512]{3,2,0,1:T(8,128)(2,1)}, u32[]{:S(2)}, u32[]{:S(2)}) async-start(bf16[4,32,8,512]{3,2,0,1:T(8,128)(2,1)} %reshape.114), calls=%async_computation.1 | async-start | bytes 2097152 | tf_op jit(solution)/shard_map/all_to_all | solution.py:57
  105.9 32.2 %all-to-all-start.3 = ((bf16[8,4,32,512]{3,1,0,2:T(4,128)(2,1)}), bf16[8,4,32,512]{3,1,0,2:T(4,128)(2,1)S(1)}, u32[]{:S(2)}, u32[]{:S(2)}) async-start(bf16[8,4,32,512]{3,1,0,2:T(4,128)(2,1)} %reshape.115), calls=%async_computation.3 | async-start | bytes 2097152 | tf_op jit(solution)/shard_map/all_to_all | solution.py:61
  119.8 5.5 %copy-start.6 = (bf16[2,16,32,8,64]{4,3,2,1,0:T(8,128)(2,1)S(1)}, bf16[2,16,32,8,64]{4,3,2,1,0:T(8,128)(2,1)}, u32[]{:S(2)}) copy-start(bf16[2,16,32,8,64]{4,3,2,1,0:T(8,128)(2,1)} %reshape.94) | copy-start | bytes 3145732
  138.1 1.6 %copy-start.4 = (f32[8,4,4,8,512]{4,3,2,1,0:T(8,128)S(1)}, f32[8,4,4,8,512]{4,3,2,1,0:T(8,128)}, u32[]{:S(2)}) copy-start(f32[8,4,4,8,512]{4,3,2,1,0:T(8,128)} %copy.57) | copy-start | bytes 6291460
  138.7 1.4 copy-start.2
  138.8 2.1 %copy-start.3 = (f32[2,16,4,8,512]{4,3,2,1,0:T(8,128)S(1)}, f32[2,16,4,8,512]{4,3,2,1,0:T(8,128)}, u32[]{:S(2)}) copy-start(f32[2,16,4,8,512]{4,3,2,1,0:T(8,128)} %reshape.108) | copy-start | bytes 6291460
  138.8 2.1 %copy-start.7 = (bf16[512,512]{1,0:T(8,128)(2,1)S(1)}, bf16[512,512]{1,0:T(8,128)(2,1)}, u32[]{:S(2)}) copy-start(bf16[512,512]{1,0:T(8,128)(2,1)} %param.7) | copy-start | bytes 1572868
  140.9 1.7 %copy-start.1 = (bf16[512,1536]{1,0:T(8,128)(2,1)S(1)}, bf16[512,1536]{1,0:T(8,128)(2,1)}, u32[]{:S(2)}) copy-start(bf16[512,1536]{1,0:T(8,128)(2,1)} %param.6) | copy-start | bytes 4718596
where the time goes:
time: 144 us; the launch traced here: 143 us
  local copies, waits for them, and re-layouts  64.7 us (45%)
  matrix products  30.6 us (21%)
  other arithmetic  24.1 us (17%)
  starting transfers between devices  20 us (14%)
  waiting for transfers between devices  2.99 us (2%)
    sub x3, other arithmetic, attend(): expo = jnp.exp(scores - highest)  19 us
    dot_general x3, matrix products, attend(): jnp.einsum(form_scores, queries, key_part, preferred_element_type=jnp.flo...  15.1 us
    convert_element_type x4, local copies, waits for them, and re-layouts, attend(): return mixed.reshape(shape[:-1] + (width,)).astype(jnp.bfloat16)  12.6 us
    reshape x3, local copies, waits for them, and re-layouts, attend(): key_part = triple[..., width:2 * width].reshape(split)  11.7 us
    reshape x3, local copies, waits for them, and re-layouts, attend(): queries = triple[..., :width].reshape(split)  11.7 us
    reshape x3, local copies, waits for them, and re-layouts, attend(): values = triple[..., 2 * width:].reshape(split)  8.01 us
    convert_element_type x2, local copies, waits for them, and re-layouts, body(): along_time.astype(jnp.float32)  7.96 us
    dot_general x3, matrix products, attend(): jnp.einsum(form_mix, weights, values, preferred_element_type=jnp.float32)  7.25 us
  transfers between devices with their start and end apart: 4, of which 1 were waited for; matrix products, arithmetic and copies ran while one was open for 78% of the time, Pallas kernels for 0%

commit v1 on v0

v1 whole, which is shorter than its diff:
```python
import functools
import math

import jax
import jax.numpy as jnp
from jax import lax
from jax.experimental import pallas as pl
from jax.experimental.pallas import tpu as pltpu
from jax.sharding import PartitionSpec as P

HEADS = 8
MASKED = -1e30
Y_CHUNKS = 2
VMEM = pl.BlockSpec(memory_space=pltpu.VMEM)
ANY = pl.BlockSpec(memory_space=pl.ANY)
PARAMS = pltpu.CompilerParams(vmem_limit_bytes=48 * 1024 * 1024)


def normalize(field, gain):
    scale = lax.rsqrt(jnp.mean(field * field, axis=-1, keepdims=True) + 1e-05)
    return (field * scale * gain).astype(jnp.bfloat16)


def line_bias(block, line_of):
    key_at = lax.broadcasted_iota(jnp.int32, (block, 2 * block), 0)
    query_at = lax.rem(lax.broadcasted_iota(jnp.int32, (block, 2 * block), 1), block)
    return jnp.where(line_of(key_at) == line_of(query_at), 0.0, MASKED).astype(jnp.float32)


def project(normed_ref, w_ref, w_values_ref, qk_ref, values_ref):
    total, width = normed_ref.shape
    step = min(256, total)
    for at in range(0, total, step):
        rows = normed_ref[at : at + step]
        qk_ref[at : at + step] = jnp.dot(
            rows, w_ref[:, : 2 * width], preferred_element_type=jnp.float32
        ).astype(jnp.bfloat16)
        values_ref[:, at : at + step] = lax.dot_general(
            w_values_ref[...], rows, (((1,), (1,)), ((), ())), preferred_element_type=jnp.float32
        ).astype(jnp.bfloat16)


def attend(qk, values, bias):
    block, width = qk.shape[0], qk.shape[1] // 2
    size = width // HEADS
    factor = math.log2(math.e) / math.sqrt(size)
    lane = lax.broadcasted_iota(jnp.int32, (block, 2 * size), 1)
    mixed = []
    for at in range(0, width, 2 * size):
        queries = qk[:, at : at + 2 * size]
        key_part = qk[:, width + at : width + at + 2 * size]
        zero = jnp.zeros_like(queries)
        pair = jnp.concatenate(
            [jnp.where(lane < size, queries, zero), jnp.where(lane < size, zero, queries)], axis=0
        )
        scores = lax.dot_general(
            key_part, pair, (((1,), (1,)), ((), ())), preferred_element_type=jnp.float32
        )
        scores = scores + bias
        expo = jnp.exp2((scores - jnp.max(scores, axis=0, keepdims=True)) * factor)
        inverse = 1.0 / jnp.sum(expo, axis=0, keepdims=True)
        expo = expo.astype(jnp.bfloat16)
        for head in range(2):
            rows = slice(at + head * size, at + (head + 1) * size)
            columns = slice(head * block, (head + 1) * block)
            summed = jnp.dot(values[rows], expo[:, columns], preferred_element_type=jnp.float32)
            mixed.append(summed * inverse[:, columns])
    return jnp.concatenate(mixed, axis=0)


def attention_scratch(total, block, width):
    return [
        pltpu.VMEM((total, width), jnp.bfloat16),
        pltpu.VMEM((total, 2 * width), jnp.bfloat16),
        pltpu.VMEM((width, total), jnp.bfloat16),
        pltpu.VMEM((block, 2 * block), jnp.float32),
    ]


def time_kernel(
    gain_ref, w_ref, w_values_ref, tokens_ref, out_ref, normed_ref, qk_ref, values_ref, bias_ref
):
    batch, steps, cells_x, cells_y, width = tokens_ref.shape
    block = steps * cells_y
    bias_ref[...] = line_bias(block, lambda at: lax.rem(at, cells_y))
    places = [(b, x) for b in range(batch) for x in range(cells_x)]
    for index, (b, x) in enumerate(places):
        field = tokens_ref[b, :, x].astype(jnp.float32).reshape(block, width)
        normed_ref[index * block : (index + 1) * block] = normalize(field, gain_ref[...])
    project(normed_ref, w_ref, w_values_ref, qk_ref, values_ref)
    for index, (b, x) in enumerate(places):
        rows = slice(index * block, (index + 1) * block)
        out = attend(qk_ref[rows], values_ref[:, rows], bias_ref[...]).T
        out_ref[b, :, x] = out.reshape(steps, cells_y, width).astype(jnp.bfloat16)


def attend_time(tokens, gain, w_qkv, w_values):
    batch, steps, cells_x, cells_y, width = tokens.shape
    block = steps * cells_y
    return pl.pallas_call(
        time_kernel,
        out_shape=jax.ShapeDtypeStruct(tokens.shape, tokens.dtype),
        in_specs=[VMEM] * 4,
        out_specs=VMEM,
        scratch_shapes=attention_scratch(batch * cells_x * block, block, width),
        compiler_params=PARAMS,
        name="attend_time",
    )(gain, w_qkv, w_values, tokens)


def planes_attention(parts, outs, line_of, gain_ref, w_ref, w_values_ref, scratch):
    normed_ref, qk_ref, values_ref, bias_ref = scratch
    block = bias_ref.shape[0]
    planes = normed_ref.shape[0] // block
    bias_ref[...] = line_bias(block, line_of)
    for plane in range(planes):
        field = jnp.concatenate([part(plane) for part in parts], axis=0)
        normed_ref[plane * block : (plane + 1) * block] = normalize(field, gain_ref[...])
    project(normed_ref, w_ref, w_values_ref, qk_ref, values_ref)
    for plane in range(planes):
        rows = slice(plane * block, (plane + 1) * block)
        out = attend(qk_ref[rows], values_ref[:, rows], bias_ref[...]).T
        each = block // len(parts)
        for index, put in enumerate(outs):
            put(plane, out[index * each : (index + 1) * each])


def y_kernel(count, gain_ref, w_ref, w_values_ref, *refs):
    pieces, results, scratch = refs[:count], refs[count : 2 * count], refs[2 * count :]
    _, cells_x, cells_y, width = pieces[0].shape

    def part(ref):
        return lambda plane: ref[plane].astype(jnp.float32).reshape(cells_x * cells_y, width)

    def put(ref):
        def store(plane, value):
            ref[plane] = value.reshape(cells_x, cells_y, width).astype(jnp.bfloat16)

        return store

    planes_attention(
        [part(ref) for ref in pieces],
        [put(ref) for ref in results],
        lambda at: lax.rem(lax.div(at, cells_y), cells_x),
        gain_ref,
        w_ref,
        w_values_ref,
        scratch,
    )


def attend_y(pieces, gain, w_qkv, w_values):
    count = len(pieces)
    planes, cells_x, cells_y, width = pieces[0].shape
    block = count * cells_x * cells_y
    return pl.pallas_call(
        functools.partial(y_kernel, count),
        out_shape=[jax.ShapeDtypeStruct(piece.shape, piece.dtype) for piece in pieces],
        in_specs=[VMEM] * (3 + count),
        out_specs=[VMEM] * count,
        scratch_shapes=attention_scratch(planes * block, block, width),
        compiler_params=PARAMS,
        name="attend_y",
    )(gain, w_qkv, w_values, *pieces)


def x_kernel(count, gain_ref, w_ref, w_values_ref, *refs):
    pieces, sibling = refs[:count], refs[count]
    results, scratch = refs[count + 1 : 2 * count + 1], refs[2 * count + 1 :]
    _, _, cells_x, cells_y, width = pieces[0].shape
    core = lax.rem(lax.axis_index("gx"), 2)

    def part(ref, index):
        return lambda plane: ref[index, plane].astype(jnp.float32).reshape(cells_x * cells_y, width)

    def put(ref, index):
        def store(plane, value):
            ref[index, plane] = value.reshape(cells_x, cells_y, width).astype(jnp.bfloat16)

        return store

    planes_attention(
        [part(ref, core) for ref in pieces] + [part(sibling, at) for at in range(count)],
        [put(ref, 0) for ref in results] + [put(ref, 1) for ref in results],
        lambda at: lax.rem(at, cells_y),
        gain_ref,
        w_ref,
        w_values_ref,
        scratch,
    )


def attend_x(pieces, sibling, gain, w_qkv, w_values):
    count = len(pieces)
    _, planes, cells_x, cells_y, width = pieces[0].shape
    block = 2 * count * cells_x * cells_y
    return pl.pallas_call(
        functools.partial(x_kernel, count),
        out_shape=[jax.ShapeDtypeStruct(piece.shape, piece.dtype) for piece in pieces],
        in_specs=[VMEM] * (4 + count),
        out_specs=[VMEM] * count,
        scratch_shapes=attention_scratch(planes * block, block, width),
        compiler_params=PARAMS,
        name="attend_x",
    )(gain, w_qkv, w_values, *pieces, sibling)


def base_kernel(count, along_time_ref, *refs):
    pieces, sibling, out_ref = refs[:count], refs[count], refs[count + 1]
    planes = pieces[0].shape[1]
    device = lax.axis_index("gx")
    chip, core = device // 2, lax.rem(device, 2)
    for index in range(count):
        for lane, source in ((core, pieces[index].at[0]), (1 - core, sibling.at[index])):
            at = pl.ds(((chip ^ index) * 2 + lane) * planes, planes)
            out_ref[at] = along_time_ref[at].astype(jnp.float32) + source[...].astype(jnp.float32)


def add_x(along_time, pieces, sibling):
    return pl.pallas_call(
        functools.partial(base_kernel, len(pieces)),
        out_shape=jax.ShapeDtypeStruct(along_time.shape, jnp.float32),
        in_specs=[VMEM] * (2 + len(pieces)),
        out_specs=VMEM,
        compiler_params=PARAMS,
        name="add_x",
    )(along_time, *pieces, sibling)


def final_kernel(count, chunk, w_ref, tokens_ref, base_ref, *refs):
    pieces = refs[:count]
    out_ref, held, sems = refs[-3:]
    planes, cells_x, cells_y, width = pieces[0].shape
    group = tokens_ref.shape[0] // count
    me = lax.axis_index("gy")
    copies = []
    for index in range(count):
        at = pl.ds((me ^ index) * group + chunk * planes, planes)
        mixed = base_ref[at] + pieces[index][...].astype(jnp.float32)
        mixed = mixed.reshape(planes * cells_x * cells_y, width).astype(jnp.bfloat16)
        update = jnp.dot(mixed, w_ref[...], preferred_element_type=jnp.float32)
        field = tokens_ref[at].astype(jnp.float32)
        held[index] = (field + update.reshape(field.shape)).astype(jnp.bfloat16)
        copies.append(pltpu.make_async_copy(held.at[index], out_ref.at[at], sems.at[index]))
        copies[-1].start()
    for copy in copies:
        copy.wait()


def finish(chunk, w_out, tokens, base, pieces, result):
    count = len(pieces)
    earlier = [] if result is None else [result]
    return pl.pallas_call(
        functools.partial(final_kernel, count, chunk),
        out_shape=jax.ShapeDtypeStruct(tokens.shape, tokens.dtype),
        in_specs=[VMEM] * (3 + count) + [ANY] * len(earlier),
        out_specs=ANY,
        scratch_shapes=[
            pltpu.VMEM((count,) + pieces[0].shape, tokens.dtype),
            pltpu.SemaphoreType.DMA((count,)),
        ],
        input_output_aliases={3 + count: 0} if earlier else {},
        compiler_params=PARAMS,
        name="finish",
    )(w_out, tokens, base, *pieces, *earlier)


def exchange(value, axis, size, flip):
    return lax.ppermute(value, axis, [(at, at ^ flip) for at in range(size)])


def body(count_x, count_y, tokens, norm_gain, w_qkv, w_out):
    batch, steps, cells_x, cells_y, width = tokens.shape
    lines = batch * steps
    plane_shape = (cells_x, cells_y, width)
    gain = norm_gain.reshape(1, width)
    chips = count_x // 2
    device_x, device_y = lax.axis_index("gx"), lax.axis_index("gy")
    chip, core = device_x // 2, lax.rem(device_x, 2)
    chunks = math.gcd(Y_CHUNKS, lines // count_y)
    chunk_planes = lines // count_y // chunks

    by_y = tokens.reshape((count_y, chunks, chunk_planes) + plane_shape)
    y_pieces = []
    for chunk in range(chunks):
        pieces = [by_y[device_y ^ flip, chunk] for flip in range(count_y)]
        y_pieces.append(
            [p if flip == 0 else exchange(p, "gy", count_y, flip) for flip, p in enumerate(pieces)]
        )
    by_x = tokens.reshape((chips, 2, lines // count_x) + plane_shape)
    x_pieces = [by_x[chip ^ flip] for flip in range(chips)]
    x_pieces = [
        p if flip == 0 else exchange(p, "gx", count_x, 2 * flip) for flip, p in enumerate(x_pieces)
    ]
    sibling = exchange(jnp.stack([p[1 - core] for p in x_pieces]), "gx", count_x, 1)

    w_values = w_qkv[:, 2 * width :].T
    along_time = attend_time(tokens, gain, w_qkv, w_values).reshape((lines,) + plane_shape)

    x_pieces = attend_x(x_pieces, sibling, gain, w_qkv, w_values)
    x_pieces = [
        p if flip == 0 else exchange(p, "gx", count_x, 2 * flip) for flip, p in enumerate(x_pieces)
    ]
    sibling = exchange(jnp.stack([p[1] for p in x_pieces]), "gx", count_x, 1)
    base = add_x(along_time, x_pieces, sibling)

    result = None
    flat = tokens.reshape((lines,) + plane_shape)
    returned = []
    for pieces in y_pieces:
        pieces = attend_y(pieces, gain, w_qkv, w_values)
        returned.append(
            [p if flip == 0 else exchange(p, "gy", count_y, flip) for flip, p in enumerate(pieces)]
        )
    for chunk, pieces in enumerate(returned):
        result = finish(chunk, w_out, flat, base, pieces, result)
    return result.reshape(tokens.shape)


def solution(mesh):
    placed = (P(None, None, "gx", "gy", None), P(), P(), P())
    return jax.shard_map(
        functools.partial(body, mesh.shape["gx"], mesh.shape["gy"]),
        mesh=mesh,
        in_specs=placed,
        out_specs=P(None, None, "gx", "gy", None),
        check_vma=False,
    )
```

time: 144 us -> 99.1 us (0.69)
  local copies, waits for them, and re-layouts: 64.7 us -> 8.72 us
  waiting for transfers between devices: 2.99 us -> 38.7 us
  matrix products: 30.6 us -> 0 us
  other arithmetic: 24.1 us -> 0.94 us
  Pallas kernels: 0 us -> 19.6 us
  starting transfers between devices: 20 us -> 30.5 us
    ppermute x0 -> x20, waiting for transfers between devices: none -> 38.7 us  [exchange(): return lax.ppermute(value, axis, [(at, at ^ flip) for at in range(size)])]
    reshape x9 -> x0, local copies, waits for them, and re-layouts: 31.4 us -> none  [the longest x3 11.7 us: attend(): key_part = triple[..., width:2 * width].reshape(split)]
    dot_general x10 -> x0, matrix products: 30.6 us -> none  [the longest x3 15.1 us: attend(): jnp.einsum(form_scores, queries, key_part, preferred_element_type=jnp.flo...]
    ppermute x0 -> x20, starting transfers between devices: none -> 30.5 us  [exchange(): return lax.ppermute(value, axis, [(at, at ^ flip) for at in range(size)])]
    convert_element_type x8 -> x0, local copies, waits for them, and re-layouts: 22.2 us -> none  [the longest x4 12.6 us: attend(): return mixed.reshape(shape[:-1] + (width,)).astype(jnp.bfloat16)]
    all_to_all x4 -> x0, starting transfers between devices: 20 us -> none  [the longest x1 5.3 us: body(): lax.all_to_all(outgoing, 'gy', split_axis=0, concat_axis=2, tiled=True)]
    pallas_call x0 -> x7, Pallas kernels: none -> 19.6 us  [the longest x1 8.31 us: attend_x(): pl.pallas_call(functools.partial(x_kernel, count), out_shape=[jax.ShapeDt...]
    sub x3 -> x0, other arithmetic: 19 us -> none  [attend(): expo = jnp.exp(scores - highest)]
  transfers between devices with their start and end apart: 4 -> 20, of which waited for: 1 -> 10; matrix products, arithmetic and copies ran while one was open for 78% -> 4% of each run, Pallas kernels for 0% -> 10%
where the time goes in v1:
time: 99.1 us; the launch traced here: 98.8 us
  waiting for transfers between devices  38.7 us (39%)
  starting transfers between devices  30.5 us (31%)
  Pallas kernels  19.6 us (20%)
  local copies, waits for them, and re-layouts  8.72 us (9%)
    ppermute x20, waiting for transfers between devices, exchange(): return lax.ppermute(value, axis, [(at, at ^ flip) for at in range(size)])  38.7 us
    ppermute x20, starting transfers between devices, exchange(): return lax.ppermute(value, axis, [(at, at ^ flip) for at in range(size)])  30.5 us
    pallas_call x1, Pallas kernels, attend_x(): pl.pallas_call(functools.partial(x_kernel, count), out_shape=[jax.ShapeDt...  8.31 us
    pallas_call x2, Pallas kernels, attend_y(): pl.pallas_call(functools.partial(y_kernel, count), out_shape=[jax.ShapeDt...  4.76 us
    pallas_call x1, Pallas kernels, attend_time(): pl.pallas_call(time_kernel, out_shape=jax.ShapeDtypeStruct(tokens.shape,...  3.9 us
    unnamed x25, local copies, waits for them, and re-layouts  2.83 us
    dynamic_slice x3, local copies, waits for them, and re-layouts, body(): p[1 - core]  2.75 us
    pallas_call x2, Pallas kernels, finish(): pl.pallas_call(functools.partial(final_kernel, count, chunk), out_shape=j...  2.32 us
  transfers between devices with their start and end apart: 20, of which 10 were waited for; matrix products, arithmetic and copies ran while one was open for 4% of the time, Pallas kernels for 10%

profile of v1, /device:TPU:0, one launch (start us, length us, event | category | flops | bytes accessed | tf_op | source)
XLA Modules:
  0.0 98.8 jit_solution(16900098675517142778)
XLA Ops:
  0.0 2.2 %dynamic-slice_bitcast_fusion = (bf16[2,4,4,8,512]{4,3,2,1,0:T(8,128)(2,1)}, bf16[2,4,4,8,512]{4,3,2,1,0:T(8,128)(2,1)}, bf16[2,4,4,8,512]{4,3,2,1,0:T(8,128)(2,1)}, bf16[2,4,4,8,512]{4,3,2,1,0:T(8,128)(2,1)S(1)}) fusion(bf16[4,2,4,4,8,512]{5,4,3,2,1,0:T(8,128)(2,1)} %bitcast.32, s32[]{:T(128)S(6)} %select_n.47, s32[]{:T(128)S(6)} %select_n.46, ...), kind=kLoop, calls=%fused_computation.2 | loop fusion | bytes 2097168 | tf_op jit(solution)/shard_map/squeeze | solution.py:291
  2.2 3.9 %collective-permute-start.2 = (bf16[2,4,4,8,512]{4,3,2,1,0:T(8,128)(2,1)}, bf16[2,4,4,8,512]{4,3,2,1,0:T(8,128)(2,1)}, u32[]{:S(2)}, u32[]{:S(2)}) collective-permute-start(bf16[2,4,4,8,512]{4,3,2,1,0:T(8,128)(2,1)} %get-tuple-element.38), channel_id=1, source_target_pairs={{0,24},{4,28},{8,16},{12,20},{16,8},{20,12},{24,0},{28,4},{1,25},{... | collective-permute-start | bytes 786440 | tf_op jit(solution)/shard_map/ppermute | solution.py:269
  6.1 0.5 collective-permute-start.1
  6.6 0.1 collective-permute-start
  6.6 0.0 copy-done.1
  6.6 0.9 dynamic-slice_bitcast_fusion.4
  7.6 6.0 %collective-permute-done.2.refs_3_ = bf16[2,4,4,8,512]{4,3,2,1,0:T(8,128)(2,1)} collective-permute-done((bf16[2,4,4,8,512]{4,3,2,1,0:T(8,128)(2,1)}, bf16[2,4,4,8,512]{4,3,2,1,0:T(8,128)(2,1)}, u32[]{:S(2)}, u32[]{:S(2)}) %collective-permute-start.2) | collective-permute-done | bytes 262176 | tf_op jit(solution)/shard_map/ppermute | solution.py:269
  13.6 0.9 constant_dynamic-slice_fusion
  14.5 3.8 %collective-permute-done.1.refs_2_ = bf16[2,4,4,8,512]{4,3,2,1,0:T(8,128)(2,1)} collective-permute-done((bf16[2,4,4,8,512]{4,3,2,1,0:T(8,128)(2,1)}, bf16[2,4,4,8,512]{4,3,2,1,0:T(8,128)(2,1)}, u32[]{:S(2)}, u32[]{:S(2)}) %collective-permute-start.1) | collective-permute-done | bytes 262176 | tf_op jit(solution)/shard_map/ppermute | solution.py:269
  18.3 0.9 constant_dynamic-slice_fusion.1
  19.2 0.0 collective-permute-done.refs_1_
  19.2 0.9 constant_dynamic-slice_fusion.2
  20.1 0.9 pad_maximum_fusion
  21.0 0.0 collective-permute-start.3
  21.0 0.0 slice-done
  21.0 1.0 %copy.7 = bf16[512,512]{0,1:T(8,128)(2,1)} copy(bf16[512,512]{1,0:T(8,128)(2,1)S(1)} %slice-done) | data formatting | bytes 1048576
  22.0 1.2 %collective-permute-done.3.refs_4_ = bf16[4,4,4,8,512]{4,3,2,1,0:T(8,128)(2,1)} collective-permute-done((bf16[4,4,4,8,512]{4,3,2,1,0:T(8,128)(2,1)}, bf16[4,4,4,8,512]{4,3,2,1,0:T(8,128)(2,1)}, u32[]{:S(2)}, u32[]{:S(2)}) %collective-permute-start.3) | collective-permute-done | bytes 524320 | tf_op jit(solution)/shard_map/ppermute | solution.py:269
  23.3 0.0 copy-done
  23.3 0.0 copy-done.5
  23.3 1.0 %copy-done.2 = bf16[512,512]{0,1:T(8,128)(2,1)S(1)} copy-done((bf16[512,512]{0,1:T(8,128)(2,1)S(1)}, bf16[512,512]{0,1:T(8,128)(2,1)}, u32[]{:S(2)}) %copy-start.2) | copy-done | bytes 524312
  24.4 8.3 %attend_x.1 = (bf16[2,4,4,8,512]{4,3,2,1,0:T(8,128)(2,1)S(1)}, bf16[2,4,4,8,512]{4,3,2,1,0:T(8,128)(2,1)S(1)}, bf16[2,4,4,8,512]{4,3,2,1,0:T(8,128)(2,1)S(1)}, bf16[2,4,4,8,512]{4,3,2,1,0:T(8,128)(2,1)S(1)}) custom-call(f32[1,512]{1,0:T(1,128)S(1)} %bitcast.41, bf16[512,1536]{1,0:T(8,128)(2,1)S(1)} %copy-done, bf16[512,512]{1,0:T(8,128)(2,1)S(1)} %bitcast.36, ...), custom_call_target="tpu_custom_call" | custom-call | tf_op jit(solution)/shard_map/attend_x/pallas_call | solution.py:197
  32.7 1.7 %collective-permute-start.4 = (bf16[2,4,4,8,512]{4,3,2,1,0:T(8,128)(2,1)S(1)}, bf16[2,4,4,8,512]{4,3,2,1,0:T(8,128)(2,1)S(1)}, u32[]{:S(2)}, u32[]{:S(2)}) collective-permute-start(bf16[2,4,4,8,512]{4,3,2,1,0:T(8,128)(2,1)S(1)} %get-tuple-element.18), channel_id=1, source_target_pairs={{0,8},{4,12},{8,0},{12,4},{16,24},{20,28},{24,16},{28,20},{1,9},{5... | collective-permute-start | bytes 786440 | tf_op jit(solution)/shard_map/ppermute | solution.py:269
  34.4 0.6 collective-permute-start.5
  35.0 1.2 %collective-permute-start.6 = (bf16[2,4,4,8,512]{4,3,2,1,0:T(8,128)(2,1)S(1)}, bf16[2,4,4,8,512]{4,3,2,1,0:T(8,128)(2,1)S(1)}, u32[]{:S(2)}, u32[]{:S(2)}) collective-permute-start(bf16[2,4,4,8,512]{4,3,2,1,0:T(8,128)(2,1)S(1)} %get-tuple-element.20), channel_id=1, source_target_pairs={{0,24},{4,28},{8,16},{12,20},{16,8},{20,12},{24,0},{28,4},{1,25},{... | collective-permute-start | bytes 786440 | tf_op jit(solution)/shard_map/ppermute | solution.py:269
  36.2 5.6 %collective-permute-done.4.refs_1_ = bf16[2,4,4,8,512]{4,3,2,1,0:T(8,128)(2,1)S(1)} collective-permute-done((bf16[2,4,4,8,512]{4,3,2,1,0:T(8,128)(2,1)S(1)}, bf16[2,4,4,8,512]{4,3,2,1,0:T(8,128)(2,1)S(1)}, u32[]{:S(2)}, u32[]{:S(2)}) %collective-permute-start.4) | collective-permute-done | bytes 262176 | tf_op jit(solution)/shard_map/ppermute | solution.py:269
  41.9 6.2 %collective-permute-done.5.refs_2_ = bf16[2,4,4,8,512]{4,3,2,1,0:T(8,128)(2,1)S(1)} collective-permute-done((bf16[2,4,4,8,512]{4,3,2,1,0:T(8,128)(2,1)S(1)}, bf16[2,4,4,8,512]{4,3,2,1,0:T(8,128)(2,1)S(1)}, u32[]{:S(2)}, u32[]{:S(2)}) %collective-permute-start.5) | collective-permute-done | bytes 262176 | tf_op jit(solution)/shard_map/ppermute | solution.py:269
  48.1 0.0 collective-permute-done.6.refs_3_
  48.2 0.1 pad_maximum_fusion.1
  48.2 0.1 collective-permute-start.7
  48.3 3.7 %collective-permute-start.16 = (bf16[4,4,8,512]{3,2,1,0:T(8,128)(2,1)S(1)}, bf16[4,4,8,512]{3,2,1,0:T(8,128)(2,1)S(1)}, u32[]{:S(2)}, u32[]{:S(2)}) collective-permute-start(bf16[4,4,8,512]{3,2,1,0:T(8,128)(2,1)S(1)} %copy-done.11), channel_id=1, source_target_pairs={{0,3},{1,2},{2,1},{3,0},{4,7},{5,6},{6,5},{7,4},{8,11},{9,10},{10,... | collective-permute-start | bytes 393224 | tf_op jit(solution)/shard_map/ppermute | solution.py:269
  52.0 0.0 collective-permute-start.15
  52.0 0.0 copy-done.9
  52.0 0.8 collective-permute-start.14
  52.8 0.0 copy-done.8
  52.8 3.6 %collective-permute-start.10 = (bf16[4,4,8,512]{3,2,1,0:T(8,128)(2,1)S(1)}, bf16[4,4,8,512]{3,2,1,0:T(8,128)(2,1)S(1)}, u32[]{:S(2)}, u32[]{:S(2)}) collective-permute-start(bf16[4,4,8,512]{3,2,1,0:T(8,128)(2,1)S(1)} %copy-done.8), channel_id=1, source_target_pairs={{0,3},{1,2},{2,1},{3,0},{4,7},{5,6},{6,5},{7,4},{8,11},{9,10},{10,... | collective-permute-start | bytes 393224 | tf_op jit(solution)/shard_map/ppermute | solution.py:269
  56.4 0.2 collective-permute-done.16.refs_3_
  56.6 6.3 %collective-permute-start.9 = (bf16[4,4,8,512]{3,2,1,0:T(8,128)(2,1)S(1)}, bf16[4,4,8,512]{3,2,1,0:T(8,128)(2,1)S(1)}, u32[]{:S(2)}, u32[]{:S(2)}) collective-permute-start(bf16[4,4,8,512]{3,2,1,0:T(8,128)(2,1)S(1)} %copy-done.7), channel_id=1, source_target_pairs={{0,2},{1,3},{2,0},{3,1},{4,6},{5,7},{6,4},{7,5},{8,10},{9,11},{10,... | collective-permute-start | bytes 393224 | tf_op jit(solution)/shard_map/ppermute | solution.py:269
  62.9 6.8 %collective-permute-done.15.refs_2_ = bf16[4,4,8,512]{3,2,1,0:T(8,128)(2,1)S(1)} collective-permute-done((bf16[4,4,8,512]{3,2,1,0:T(8,128)(2,1)S(1)}, bf16[4,4,8,512]{3,2,1,0:T(8,128)(2,1)S(1)}, u32[]{:S(2)}, u32[]{:S(2)}) %collective-permute-start.15) | collective-permute-done | bytes 131104 | tf_op jit(solution)/shard_map/ppermute | solution.py:269
  69.7 0.0 collective-permute-start.8
  69.8 0.0 collective-permute-done.14.refs_1_
  69.8 2.4 %attend_y.3 = (bf16[4,4,8,512]{3,2,1,0:T(8,128)(2,1)S(1)}, bf16[4,4,8,512]{3,2,1,0:T(8,128)(2,1)S(1)}, bf16[4,4,8,512]{3,2,1,0:T(8,128)(2,1)S(1)}, bf16[4,4,8,512]{3,2,1,0:T(8,128)(2,1)S(1)}) custom-call(f32[1,512]{1,0:T(1,128)S(1)} %bitcast.42, bf16[512,1536]{1,0:T(8,128)(2,1)S(1)} %copy-done, bf16[512,512]{1,0:T(8,128)(2,1)S(1)} %bitcast.37, ...), custom_call_target="tpu_custom_call" | custom-call | tf_op jit(solution)/shard_map/attend_y/pallas_call | solution.py:156
  72.2 2.1 %collective-permute-start.17 = (bf16[4,4,8,512]{3,2,1,0:T(8,128)(2,1)S(1)}, bf16[4,4,8,512]{3,2,1,0:T(8,128)(2,1)S(1)}, u32[]{:S(2)}, u32[]{:S(2)}) collective-permute-start(bf16[4,4,8,512]{3,2,1,0:T(8,128)(2,1)S(1)} %get-tuple-element.26), channel_id=1, source_target_pairs={{0,1},{1,0},{2,3},{3,2},{4,5},{5,4},{6,7},{7,6},{8,9},{9,8},{10,11... | collective-permute-start | bytes 393224 | tf_op jit(solution)/shard_map/ppermute | solution.py:269
  74.2 0.0 collective-permute-done.10.refs_3_
  74.2 1.1 %collective-permute-start.18 = (bf16[4,4,8,512]{3,2,1,0:T(8,128)(2,1)S(1)}, bf16[4,4,8,512]{3,2,1,0:T(8,128)(2,1)S(1)}, u32[]{:S(2)}, u32[]{:S(2)}) collective-permute-start(bf16[4,4,8,512]{3,2,1,0:T(8,128)(2,1)S(1)} %get-tuple-element.27), channel_id=1, source_target_pairs={{0,2},{1,3},{2,0},{3,1},{4,6},{5,7},{6,4},{7,5},{8,10},{9,11},{10,... | collective-permute-start | bytes 393224 | tf_op jit(solution)/shard_map/ppermute | solution.py:269
  75.3 0.0 collective-permute-done.9.refs_2_
  75.3 2.1 %collective-permute-start.19 = (bf16[4,4,8,512]{3,2,1,0:T(8,128)(2,1)S(1)}, bf16[4,4,8,512]{3,2,1,0:T(8,128)(2,1)S(1)}, u32[]{:S(2)}, u32[]{:S(2)}) collective-permute-start(bf16[4,4,8,512]{3,2,1,0:T(8,128)(2,1)S(1)} %get-tuple-element.28), channel_id=1, source_target_pairs={{0,3},{1,2},{2,1},{3,0},{4,7},{5,6},{6,5},{7,4},{8,11},{9,10},{10,... | collective-permute-start | bytes 393224 | tf_op jit(solution)/shard_map/ppermute | solution.py:269
  77.5 1.9 %collective-permute-done.8.refs_1_ = bf16[4,4,8,512]{3,2,1,0:T(8,128)(2,1)S(1)} collective-permute-done((bf16[4,4,8,512]{3,2,1,0:T(8,128)(2,1)S(1)}, bf16[4,4,8,512]{3,2,1,0:T(8,128)(2,1)S(1)}, u32[]{:S(2)}, u32[]{:S(2)}) %collective-permute-start.8) | collective-permute-done | bytes 131104 | tf_op jit(solution)/shard_map/ppermute | solution.py:269
  79.4 2.4 %attend_y.2 = (bf16[4,4,8,512]{3,2,1,0:T(8,128)(2,1)S(1)}, bf16[4,4,8,512]{3,2,1,0:T(8,128)(2,1)S(1)}, bf16[4,4,8,512]{3,2,1,0:T(8,128)(2,1)S(1)}, bf16[4,4,8,512]{3,2,1,0:T(8,128)(2,1)S(1)}) custom-call(f32[1,512]{1,0:T(1,128)S(1)} %bitcast.43, bf16[512,1536]{1,0:T(8,128)(2,1)S(1)} %copy-done, bf16[512,512]{1,0:T(8,128)(2,1)S(1)} %bitcast.38, ...), custom_call_target="tpu_custom_call" | custom-call | tf_op jit(solution)/shard_map/attend_y/pallas_call | solution.py:156
  81.8 0.3 collective-permute-start.11
  82.1 4.1 %collective-permute-done.17.refs_1_ = bf16[4,4,8,512]{3,2,1,0:T(8,128)(2,1)S(1)} collective-permute-done((bf16[4,4,8,512]{3,2,1,0:T(8,128)(2,1)S(1)}, bf16[4,4,8,512]{3,2,1,0:T(8,128)(2,1)S(1)}, u32[]{:S(2)}, u32[]{:S(2)}) %collective-permute-start.17) | collective-permute-done | bytes 131104 | tf_op jit(solution)/shard_map/ppermute | solution.py:269
  86.2 0.3 collective-permute-start.12
  86.5 0.0 collective-permute-done.7.refs_4_
  86.5 2.2 %collective-permute-start.13 = (bf16[4,4,8,512]{3,2,1,0:T(8,128)(2,1)S(1)}, bf16[4,4,8,512]{3,2,1,0:T(8,128)(2,1)S(1)}, u32[]{:S(2)}, u32[]{:S(2)}) collective-permute-start(bf16[4,4,8,512]{3,2,1,0:T(8,128)(2,1)S(1)} %get-tuple-element.24), channel_id=1, source_target_pairs={{0,3},{1,2},{2,1},{3,0},{4,7},{5,6},{6,5},{7,4},{8,11},{9,10},{10,... | collective-permute-start | bytes 393224 | tf_op jit(solution)/shard_map/ppermute | solution.py:269
  88.7 3.9 %attend_time.1 = bf16[2,16,4,8,512]{4,3,2,1,0:T(8,128)(2,1)S(1)} custom-call(f32[1,512]{1,0:T(1,128)S(1)} %bitcast.44, bf16[512,1536]{1,0:T(8,128)(2,1)S(1)} %copy-done, bf16[512,512]{1,0:T(8,128)(2,1)S(1)} %bitcast.39, bf16[2,16,4,8,512]{4,3,2,1,0:T(8,128)(2,1)S(1)} %copy-done.1), custom_call_target="tpu_custom_call" | custom-call | tf_op jit(solution)/shard_map/attend_time/pallas_call | solution.py:100
  92.6 0.0 copy-start.3
  92.6 0.3 add_x.1.base_ref
  92.9 0.0 collective-permute-done.18.refs_2_
  92.9 0.0 collective-permute-done.19.refs_3_
  92.9 0.7 copy-done.3
  93.6 1.2 %finish.2.refs_4_ = bf16[32,4,8,512]{3,2,1,0:T(8,128)(2,1)} custom-call(bf16[512,512]{1,0:T(8,128)(2,1)S(1)} %copy-done.3, bf16[32,4,8,512]{3,2,1,0:T(8,128)(2,1)S(1)} %bitcast.34, f32[32,4,8,512]{3,2,1,0:T(8,128)S(1)} %add_x.1.base_ref, bf16[4,4,8,512]{3,2,1,0:T(8,128)(2,1)S(1)} %get-tuple-element.25.refs_0_, ...), custom_call_target="tpu_custom_call" | custom-call | tf_op jit(solution)/shard_map/finish/pallas_call | solution.py:253
  94.8 0.0 collective-permute-done.11.refs_1_
  94.8 2.7 %collective-permute-done.12.refs_2_ = bf16[4,4,8,512]{3,2,1,0:T(8,128)(2,1)S(1)} collective-permute-done((bf16[4,4,8,512]{3,2,1,0:T(8,128)(2,1)S(1)}, bf16[4,4,8,512]{3,2,1,0:T(8,128)(2,1)S(1)}, u32[]{:S(2)}, u32[]{:S(2)}) %collective-permute-start.12) | collective-permute-done | bytes 131104 | tf_op jit(solution)/shard_map/ppermute | solution.py:269
  97.5 0.0 collective-permute-done.13.refs_3_
  97.5 1.2 %finish.3 = bf16[32,4,8,512]{3,2,1,0:T(8,128)(2,1)} custom-call(bf16[512,512]{1,0:T(8,128)(2,1)S(1)} %copy-done.3, bf16[32,4,8,512]{3,2,1,0:T(8,128)(2,1)S(1)} %bitcast.35, f32[32,4,8,512]{3,2,1,0:T(8,128)S(1)} %add_x.1.base_ref, bf16[4,4,8,512]{3,2,1,0:T(8,128)(2,1)S(1)} %get-tuple-element.21.refs_0_, ...), custom_call_target="tpu_custom_call", output_to_operand_aliasing={{}: (7, {})} | custom-call | tf_op jit(solution)/shard_map/finish/pallas_call | solution.py:253
  (21 shorter events, 0.1 us)
Async XLA Ops:
  0.0 6.6 %copy-start.1 = (bf16[2,16,4,8,512]{4,3,2,1,0:T(8,128)(2,1)S(1)}, bf16[2,16,4,8,512]{4,3,2,1,0:T(8,128)(2,1)}, u32[]{:S(2)}) copy-start(bf16[2,16,4,8,512]{4,3,2,1,0:T(8,128)(2,1)} %tokens_ref.1) | copy-start | bytes 3145732
  2.2 11.4 %collective-permute-start.2 = (bf16[2,4,4,8,512]{4,3,2,1,0:T(8,128)(2,1)}, bf16[2,4,4,8,512]{4,3,2,1,0:T(8,128)(2,1)}, u32[]{:S(2)}, u32[]{:S(2)}) collective-permute-start(bf16[2,4,4,8,512]{4,3,2,1,0:T(8,128)(2,1)} %get-tuple-element.38), channel_id=1, source_target_pairs={{0,24},{4,28},{8,16},{12,20},{16,8},{20,12},{24,0},{28,4},{1,25},{... | collective-permute-start | bytes 786440 | tf_op jit(solution)/shard_map/ppermute | solution.py:269
  6.1 12.2 %collective-permute-start.1 = (bf16[2,4,4,8,512]{4,3,2,1,0:T(8,128)(2,1)}, bf16[2,4,4,8,512]{4,3,2,1,0:T(8,128)(2,1)}, u32[]{:S(2)}, u32[]{:S(2)}) collective-permute-start(bf16[2,4,4,8,512]{4,3,2,1,0:T(8,128)(2,1)} %get-tuple-element.39), channel_id=1, source_target_pairs={{0,16},{4,20},{8,24},{12,28},{16,0},{20,4},{24,8},{28,12},{1,17},{... | collective-permute-start | bytes 786440 | tf_op jit(solution)/shard_map/ppermute | solution.py:269
  6.6 12.6 %collective-permute-start = (bf16[2,4,4,8,512]{4,3,2,1,0:T(8,128)(2,1)}, bf16[2,4,4,8,512]{4,3,2,1,0:T(8,128)(2,1)}, u32[]{:S(2)}, u32[]{:S(2)}) collective-permute-start(bf16[2,4,4,8,512]{4,3,2,1,0:T(8,128)(2,1)} %get-tuple-element.40), channel_id=1, source_target_pairs={{0,8},{4,12},{8,0},{12,4},{16,24},{20,28},{24,16},{28,20},{1,9},{5... | collective-permute-start | bytes 786440 | tf_op jit(solution)/shard_map/ppermute | solution.py:269
  6.6 14.4 %slice-start = ((bf16[512,1536]{1,0:T(8,128)(2,1)}), bf16[512,512]{1,0:T(8,128)(2,1)S(1)}, s32[]{:S(2)}) async-start(bf16[512,1536]{1,0:T(8,128)(2,1)} %w_ref.9), calls=%async_computation | async-start | bytes 1048576 | tf_op jit(solution)/shard_map/slice | solution.py:297
  7.6 15.7 %copy-start = (bf16[512,1536]{1,0:T(8,128)(2,1)S(1)}, bf16[512,1536]{1,0:T(8,128)(2,1)}, u32[]{:S(2)}) copy-start(bf16[512,1536]{1,0:T(8,128)(2,1)} %w_ref.9) | copy-start | bytes 4718596
  7.6 15.7 %copy-start.5 = (f32[512]{0:T(512)S(1)}, f32[512]{0:T(512)}, u32[]{:S(2)}) copy-start(f32[512]{0:T(512)} %param.5) | copy-start | bytes 6148
  21.0 2.3 %collective-permute-start.3 = (bf16[4,4,4,8,512]{4,3,2,1,0:T(8,128)(2,1)}, bf16[4,4,4,8,512]{4,3,2,1,0:T(8,128)(2,1)}, u32[]{:S(2)}, u32[]{:S(2)}) collective-permute-start(bf16[4,4,4,8,512]{4,3,2,1,0:T(8,128)(2,1)} %pad_maximum_fusion), channel_id=1, source_target_pairs={{0,4},{4,0},{8,12},{12,8},{16,20},{20,16},{24,28},{28,24},{1,5},{5... | collective-permute-start | bytes 1572872 | tf_op jit(solution)/shard_map/ppermute | solution.py:269
  23.3 1.0 %copy-start.2 = (bf16[512,512]{0,1:T(8,128)(2,1)S(1)}, bf16[512,512]{0,1:T(8,128)(2,1)}, u32[]{:S(2)}) copy-start(bf16[512,512]{0,1:T(8,128)(2,1)} %copy.7) | copy-start | bytes 1572868
  24.3 24.0 %copy-start.11 = (bf16[4,4,8,512]{3,2,1,0:T(8,128)(2,1)S(1)}, bf16[4,4,8,512]{3,2,1,0:T(8,128)(2,1)}, u32[]{:S(2)}) copy-start(bf16[4,4,8,512]{3,2,1,0:T(8,128)(2,1)} %get-tuple-element.29) | copy-start | bytes 393220
  24.3 27.7 %copy-start.10 = (bf16[4,4,8,512]{3,2,1,0:T(8,128)(2,1)S(1)}, bf16[4,4,8,512]{3,2,1,0:T(8,128)(2,1)}, u32[]{:S(2)}) copy-start(bf16[4,4,8,512]{3,2,1,0:T(8,128)(2,1)} %get-tuple-element.30) | copy-start | bytes 393220
  24.3 27.7 %copy-start.9 = (bf16[4,4,8,512]{3,2,1,0:T(8,128)(2,1)S(1)}, bf16[4,4,8,512]{3,2,1,0:T(8,128)(2,1)}, u32[]{:S(2)}) copy-start(bf16[4,4,8,512]{3,2,1,0:T(8,128)(2,1)} %get-tuple-element.31) | copy-start | bytes 393220
  24.3 28.5 %copy-start.8 = (bf16[4,4,8,512]{3,2,1,0:T(8,128)(2,1)S(1)}, bf16[4,4,8,512]{3,2,1,0:T(8,128)(2,1)}, u32[]{:S(2)}) copy-start(bf16[4,4,8,512]{3,2,1,0:T(8,128)(2,1)} %get-tuple-element.33) | copy-start | bytes 393220
  24.3 32.3 %copy-start.7 = (bf16[4,4,8,512]{3,2,1,0:T(8,128)(2,1)S(1)}, bf16[4,4,8,512]{3,2,1,0:T(8,128)(2,1)}, u32[]{:S(2)}) copy-start(bf16[4,4,8,512]{3,2,1,0:T(8,128)(2,1)} %get-tuple-element.34) | copy-start | bytes 393220
  24.3 45.4 %copy-start.6 = (bf16[4,4,8,512]{3,2,1,0:T(8,128)(2,1)S(1)}, bf16[4,4,8,512]{3,2,1,0:T(8,128)(2,1)}, u32[]{:S(2)}) copy-start(bf16[4,4,8,512]{3,2,1,0:T(8,128)(2,1)} %get-tuple-element.35) | copy-start | bytes 393220
  24.4 45.4 %copy-start.4 = (bf16[4,4,8,512]{3,2,1,0:T(8,128)(2,1)S(1)}, bf16[4,4,8,512]{3,2,1,0:T(8,128)(2,1)}, u32[]{:S(2)}) copy-start(bf16[4,4,8,512]{3,2,1,0:T(8,128)(2,1)} %get-tuple-element.32.refs_0_) | copy-start | bytes 393220
  32.7 9.2 %collective-permute-start.4 = (bf16[2,4,4,8,512]{4,3,2,1,0:T(8,128)(2,1)S(1)}, bf16[2,4,4,8,512]{4,3,2,1,0:T(8,128)(2,1)S(1)}, u32[]{:S(2)}, u32[]{:S(2)}) collective-permute-start(bf16[2,4,4,8,512]{4,3,2,1,0:T(8,128)(2,1)S(1)} %get-tuple-element.18), channel_id=1, source_target_pairs={{0,8},{4,12},{8,0},{12,4},{16,24},{20,28},{24,16},{28,20},{1,9},{5... | collective-permute-start | bytes 786440 | tf_op jit(solution)/shard_map/ppermute | solution.py:269
  34.4 13.7 %collective-permute-start.5 = (bf16[2,4,4,8,512]{4,3,2,1,0:T(8,128)(2,1)S(1)}, bf16[2,4,4,8,512]{4,3,2,1,0:T(8,128)(2,1)S(1)}, u32[]{:S(2)}, u32[]{:S(2)}) collective-permute-start(bf16[2,4,4,8,512]{4,3,2,1,0:T(8,128)(2,1)S(1)} %get-tuple-element.19), channel_id=1, source_target_pairs={{0,16},{4,20},{8,24},{12,28},{16,0},{20,4},{24,8},{28,12},{1,17},{... | collective-permute-start | bytes 786440 | tf_op jit(solution)/shard_map/ppermute | solution.py:269
  35.0 13.1 %collective-permute-start.6 = (bf16[2,4,4,8,512]{4,3,2,1,0:T(8,128)(2,1)S(1)}, bf16[2,4,4,8,512]{4,3,2,1,0:T(8,128)(2,1)S(1)}, u32[]{:S(2)}, u32[]{:S(2)}) collective-permute-start(bf16[2,4,4,8,512]{4,3,2,1,0:T(8,128)(2,1)S(1)} %get-tuple-element.20), channel_id=1, source_target_pairs={{0,24},{4,28},{8,16},{12,20},{16,8},{20,12},{24,0},{28,4},{1,25},{... | collective-permute-start | bytes 786440 | tf_op jit(solution)/shard_map/ppermute | solution.py:269
  48.2 38.3 %collective-permute-start.7 = (bf16[4,4,4,8,512]{4,3,2,1,0:T(8,128)(2,1)S(1)}, bf16[4,4,4,8,512]{4,3,2,1,0:T(8,128)(2,1)S(1)}, u32[]{:S(2)}, u32[]{:S(2)}) collective-permute-start(bf16[4,4,4,8,512]{4,3,2,1,0:T(8,128)(2,1)S(1)} %pad_maximum_fusion.1), channel_id=1, source_target_pairs={{0,4},{4,0},{8,12},{12,8},{16,20},{20,16},{24,28},{28,24},{1,5},{5... | collective-permute-start | bytes 1572872 | tf_op jit(solution)/shard_map/ppermute | solution.py:269
  48.3 8.3 %collective-permute-start.16 = (bf16[4,4,8,512]{3,2,1,0:T(8,128)(2,1)S(1)}, bf16[4,4,8,512]{3,2,1,0:T(8,128)(2,1)S(1)}, u32[]{:S(2)}, u32[]{:S(2)}) collective-permute-start(bf16[4,4,8,512]{3,2,1,0:T(8,128)(2,1)S(1)} %copy-done.11), channel_id=1, source_target_pairs={{0,3},{1,2},{2,1},{3,0},{4,7},{5,6},{6,5},{7,4},{8,11},{9,10},{10,... | collective-permute-start | bytes 393224 | tf_op jit(solution)/shard_map/ppermute | solution.py:269
  52.0 17.8 %collective-permute-start.15 = (bf16[4,4,8,512]{3,2,1,0:T(8,128)(2,1)S(1)}, bf16[4,4,8,512]{3,2,1,0:T(8,128)(2,1)S(1)}, u32[]{:S(2)}, u32[]{:S(2)}) collective-permute-start(bf16[4,4,8,512]{3,2,1,0:T(8,128)(2,1)S(1)} %copy-done.10), channel_id=1, source_target_pairs={{0,2},{1,3},{2,0},{3,1},{4,6},{5,7},{6,4},{7,5},{8,10},{9,11},{10,... | collective-permute-start | bytes 393224 | tf_op jit(solution)/shard_map/ppermute | solution.py:269
  52.0 17.8 %collective-permute-start.14 = (bf16[4,4,8,512]{3,2,1,0:T(8,128)(2,1)S(1)}, bf16[4,4,8,512]{3,2,1,0:T(8,128)(2,1)S(1)}, u32[]{:S(2)}, u32[]{:S(2)}) collective-permute-start(bf16[4,4,8,512]{3,2,1,0:T(8,128)(2,1)S(1)} %copy-done.9), channel_id=1, source_target_pairs={{0,1},{1,0},{2,3},{3,2},{4,5},{5,4},{6,7},{7,6},{8,9},{9,8},{10,11... | collective-permute-start | bytes 393224 | tf_op jit(solution)/shard_map/ppermute | solution.py:269
  52.8 21.4 %collective-permute-start.10 = (bf16[4,4,8,512]{3,2,1,0:T(8,128)(2,1)S(1)}, bf16[4,4,8,512]{3,2,1,0:T(8,128)(2,1)S(1)}, u32[]{:S(2)}, u32[]{:S(2)}) collective-permute-start(bf16[4,4,8,512]{3,2,1,0:T(8,128)(2,1)S(1)} %copy-done.8), channel_id=1, source_target_pairs={{0,3},{1,2},{2,1},{3,0},{4,7},{5,6},{6,5},{7,4},{8,11},{9,10},{10,... | collective-permute-start | bytes 393224 | tf_op jit(solution)/shard_map/ppermute | solution.py:269
  56.6 18.7 %collective-permute-start.9 = (bf16[4,4,8,512]{3,2,1,0:T(8,128)(2,1)S(1)}, bf16[4,4,8,512]{3,2,1,0:T(8,128)(2,1)S(1)}, u32[]{:S(2)}, u32[]{:S(2)}) collective-permute-start(bf16[4,4,8,512]{3,2,1,0:T(8,128)(2,1)S(1)} %copy-done.7), channel_id=1, source_target_pairs={{0,2},{1,3},{2,0},{3,1},{4,6},{5,7},{6,4},{7,5},{8,10},{9,11},{10,... | collective-permute-start | bytes 393224 | tf_op jit(solution)/shard_map/ppermute | solution.py:269
  69.7 9.7 %collective-permute-start.8 = (bf16[4,4,8,512]{3,2,1,0:T(8,128)(2,1)S(1)}, bf16[4,4,8,512]{3,2,1,0:T(8,128)(2,1)S(1)}, u32[]{:S(2)}, u32[]{:S(2)}) collective-permute-start(bf16[4,4,8,512]{3,2,1,0:T(8,128)(2,1)S(1)} %copy-done.6), channel_id=1, source_target_pairs={{0,1},{1,0},{2,3},{3,2},{4,5},{5,4},{6,7},{7,6},{8,9},{9,8},{10,11... | collective-permute-start | bytes 393224 | tf_op jit(solution)/shard_map/ppermute | solution.py:269
  72.2 14.0 %collective-permute-start.17 = (bf16[4,4,8,512]{3,2,1,0:T(8,128)(2,1)S(1)}, bf16[4,4,8,512]{3,2,1,0:T(8,128)(2,1)S(1)}, u32[]{:S(2)}, u32[]{:S(2)}) collective-permute-start(bf16[4,4,8,512]{3,2,1,0:T(8,128)(2,1)S(1)} %get-tuple-element.26), channel_id=1, source_target_pairs={{0,1},{1,0},{2,3},{3,2},{4,5},{5,4},{6,7},{7,6},{8,9},{9,8},{10,11... | collective-permute-start | bytes 393224 | tf_op jit(solution)/shard_map/ppermute | solution.py:269
  74.2 18.6 %collective-permute-start.18 = (bf16[4,4,8,512]{3,2,1,0:T(8,128)(2,1)S(1)}, bf16[4,4,8,512]{3,2,1,0:T(8,128)(2,1)S(1)}, u32[]{:S(2)}, u32[]{:S(2)}) collective-permute-start(bf16[4,4,8,512]{3,2,1,0:T(8,128)(2,1)S(1)} %get-tuple-element.27), channel_id=1, source_target_pairs={{0,2},{1,3},{2,0},{3,1},{4,6},{5,7},{6,4},{7,5},{8,10},{9,11},{10,... | collective-permute-start | bytes 393224 | tf_op jit(solution)/shard_map/ppermute | solution.py:269
  75.3 17.5 %collective-permute-start.19 = (bf16[4,4,8,512]{3,2,1,0:T(8,128)(2,1)S(1)}, bf16[4,4,8,512]{3,2,1,0:T(8,128)(2,1)S(1)}, u32[]{:S(2)}, u32[]{:S(2)}) collective-permute-start(bf16[4,4,8,512]{3,2,1,0:T(8,128)(2,1)S(1)} %get-tuple-element.28), channel_id=1, source_target_pairs={{0,3},{1,2},{2,1},{3,0},{4,7},{5,6},{6,5},{7,4},{8,11},{9,10},{10,... | collective-permute-start | bytes 393224 | tf_op jit(solution)/shard_map/ppermute | solution.py:269
  81.8 13.0 %collective-permute-start.11 = (bf16[4,4,8,512]{3,2,1,0:T(8,128)(2,1)S(1)}, bf16[4,4,8,512]{3,2,1,0:T(8,128)(2,1)S(1)}, u32[]{:S(2)}, u32[]{:S(2)}) collective-permute-start(bf16[4,4,8,512]{3,2,1,0:T(8,128)(2,1)S(1)} %get-tuple-element.22), channel_id=1, source_target_pairs={{0,1},{1,0},{2,3},{3,2},{4,5},{5,4},{6,7},{7,6},{8,9},{9,8},{10,11... | collective-permute-start | bytes 393224 | tf_op jit(solution)/shard_map/ppermute | solution.py:269
  86.2 11.3 %collective-permute-start.12 = (bf16[4,4,8,512]{3,2,1,0:T(8,128)(2,1)S(1)}, bf16[4,4,8,512]{3,2,1,0:T(8,128)(2,1)S(1)}, u32[]{:S(2)}, u32[]{:S(2)}) collective-permute-start(bf16[4,4,8,512]{3,2,1,0:T(8,128)(2,1)S(1)} %get-tuple-element.23), channel_id=1, source_target_pairs={{0,2},{1,3},{2,0},{3,1},{4,6},{5,7},{6,4},{7,5},{8,10},{9,11},{10,... | collective-permute-start | bytes 393224 | tf_op jit(solution)/shard_map/ppermute | solution.py:269
  86.5 11.0 %collective-permute-start.13 = (bf16[4,4,8,512]{3,2,1,0:T(8,128)(2,1)S(1)}, bf16[4,4,8,512]{3,2,1,0:T(8,128)(2,1)S(1)}, u32[]{:S(2)}, u32[]{:S(2)}) collective-permute-start(bf16[4,4,8,512]{3,2,1,0:T(8,128)(2,1)S(1)} %get-tuple-element.24), channel_id=1, source_target_pairs={{0,3},{1,2},{2,1},{3,0},{4,7},{5,6},{6,5},{7,4},{8,11},{9,10},{10,... | collective-permute-start | bytes 393224 | tf_op jit(solution)/shard_map/ppermute | solution.py:269
  92.6 1.0 %copy-start.3 = (bf16[512,512]{1,0:T(8,128)(2,1)S(1)}, bf16[512,512]{1,0:T(8,128)(2,1)}, u32[]{:S(2)}) copy-start(bf16[512,512]{1,0:T(8,128)(2,1)} %w_ref.11) | copy-start | bytes 1572868

commit v2 on v0

v2 whole, which is shorter than its diff:
```python
import functools
import math

import jax
import jax.numpy as jnp
from jax import lax
from jax.experimental import pallas as pl
from jax.experimental.pallas import tpu as pltpu
from jax.sharding import PartitionSpec as P

HEADS = 8
MASKED = -1e30
Y_CHUNKS = 2
BLOCK = 128
LANES = 128
KERNEL_US = 5


def cost(us):
    return pl.CostEstimate(
        flops=int(1000 + us * 1.15e9),
        bytes_accessed=int(1000 + us * 3.69e6),
        transcendentals=int(us * 1e6),
    )
ANY = pl.BlockSpec(memory_space=pl.ANY)
HBM = pl.BlockSpec(memory_space=pltpu.HBM)
VMEM = pl.BlockSpec(memory_space=pltpu.VMEM)


def params(block=0):
    return pltpu.CompilerParams(vmem_limit_bytes=max(24 * 1024 * 1024, 48 * block * block))


def start_copies(pairs, sems):
    copies = [
        pltpu.make_async_copy(source, target, sems.at[at])
        for at, (source, target) in enumerate(pairs)
    ]
    for copy in copies:
        copy.start()
    return copies


def normalize(field, gain):
    scale = lax.rsqrt(jnp.mean(field * field, axis=-1, keepdims=True) + 1e-05)
    return field * scale * gain


def line_bias(block, line_of):
    key_at = lax.broadcasted_iota(jnp.int32, (block, 2 * block), 0)
    query_at = lax.rem(lax.broadcasted_iota(jnp.int32, (block, 2 * block), 1), block)
    return jnp.where(line_of(key_at) == line_of(query_at), 0.0, MASKED).astype(jnp.float32)


def project(normed_ref, w_ref, w_values_ref, qk_ref, values_ref):
    total, width = normed_ref.shape
    step = min(256, total)
    for at in range(0, total, step):
        rows = normed_ref[at : at + step]
        qk_ref[at : at + step] = jnp.dot(
            rows, w_ref[:, : 2 * width], preferred_element_type=jnp.float32
        ).astype(jnp.bfloat16)
        values_ref[:, at : at + step] = lax.dot_general(
            w_values_ref[...], rows, (((1,), (1,)), ((), ())), preferred_element_type=jnp.float32
        ).astype(jnp.bfloat16)


def attend(qk, values, bias):
    block, width = qk.shape[0], qk.shape[1] // 2
    size = width // HEADS
    factor = math.log2(math.e) / math.sqrt(size)
    lane = lax.broadcasted_iota(jnp.int32, (block, 2 * size), 1)
    mixed = []
    for at in range(0, width, 2 * size):
        queries = qk[:, at : at + 2 * size]
        key_part = qk[:, width + at : width + at + 2 * size]
        zero = jnp.zeros_like(queries)
        pair = jnp.concatenate(
            [jnp.where(lane < size, queries, zero), jnp.where(lane < size, zero, queries)], axis=0
        )
        scores = lax.dot_general(
            key_part, pair, (((1,), (1,)), ((), ())), preferred_element_type=jnp.float32
        )
        scores = scores + bias
        expo = jnp.exp2((scores - jnp.max(scores, axis=0, keepdims=True)) * factor)
        inverse = 1.0 / jnp.sum(expo, axis=0, keepdims=True)
        expo = expo.astype(jnp.bfloat16)
        for head in range(2):
            rows = slice(at + head * size, at + (head + 1) * size)
            columns = slice(head * block, (head + 1) * block)
            summed = jnp.dot(values[rows], expo[:, columns], preferred_element_type=jnp.float32)
            mixed.append(summed * inverse[:, columns])
    return jnp.concatenate(mixed, axis=0).T


def attention_kernel(plan, gain_ref, w_ref, w_values_ref, *refs):
    operands, results = refs[: plan["operands"]], refs[plan["first_result"] : plan["scratch"]]
    normed_ref, qk_ref, values_ref, bias_ref, *order_refs = refs[plan["scratch"] :]
    block, count = plan["block"], plan["count"]
    bias_ref[...] = line_bias(block, plan["line_of"])
    for index in range(count):
        plan["norm"](index, operands, gain_ref[...], normed_ref, *order_refs)
    project(normed_ref, w_ref, w_values_ref, qk_ref, values_ref)
    each = normed_ref.shape[0] // count
    for index in range(count):
        for at in range(index * each, (index + 1) * each, block):
            out = attend(qk_ref[at : at + block], values_ref[:, at : at + block], bias_ref[...])
            plan["put"](index, at - index * each, out, results, *order_refs)


def attention(plan, total, out_shapes, operands, gain, w_qkv, w_values, after, name):
    width = w_qkv.shape[0]
    block = plan["block"]
    inputs = [gain, w_qkv, w_values, *operands, *after]
    plan = dict(
        plan,
        operands=len(operands),
        first_result=len(operands) + len(after),
        scratch=len(operands) + len(after) + len(out_shapes),
    )
    bf16, f32 = jnp.bfloat16, jnp.float32
    return pl.pallas_call(
        functools.partial(attention_kernel, plan),
        out_shape=[jax.ShapeDtypeStruct(shape, bf16) for shape in out_shapes],
        in_specs=[VMEM] * (3 + len(operands)) + [ANY] * len(after),
        out_specs=[VMEM] * len(out_shapes),
        scratch_shapes=[
            pltpu.VMEM((total, width), bf16),
            pltpu.VMEM((total, 2 * width), bf16),
            pltpu.VMEM((width, total), bf16),
            pltpu.VMEM((block, 2 * block), f32),
            *[pltpu.VMEM(shape, f32) for shape in plan["order"]],
        ],
        compiler_params=params(block),
        cost_estimate=cost(KERNEL_US),
        name=name,
    )(*inputs)


def attend_time(tokens, gain, w_qkv, w_values, after=()):
    batch, steps, cells_x, cells_y, width = tokens.shape
    block = steps * cells_y
    count = batch * cells_x

    def norm(index, operands, gain, normed):
        field = operands[0][index // cells_x, :, index % cells_x].astype(jnp.float32)
        field = normalize(field.reshape(block, width), gain)
        normed[index * block : (index + 1) * block] = field.astype(jnp.bfloat16)

    def put(index, at, out, results):
        field = out.reshape(steps, cells_y, width).astype(jnp.bfloat16)
        results[0][index // cells_x, :, index % cells_x] = field

    plan = dict(
        block=block,
        count=count,
        line_of=lambda at: lax.rem(at, cells_y),
        norm=norm,
        put=put,
        order=[],
    )
    return attention(
        plan, count * block, [tokens.shape], [tokens], gain, w_qkv, w_values, after, "attend_time"
    )[0]


def attend_y(pieces, first, planes, gain, w_qkv, w_values, after=()):
    size = len(pieces)
    _, cells_x, cells_y, width = pieces[0].shape
    block = size * cells_x * cells_y

    def norm(index, operands, gain, normed):
        field = jnp.concatenate(
            [ref[first + index].astype(jnp.float32).reshape(cells_x * cells_y, width) for ref in operands],
            axis=0,
        )
        normed[index * block : (index + 1) * block] = normalize(field, gain).astype(jnp.bfloat16)

    def put(index, at, out, results):
        field = out.reshape(size, cells_x, cells_y, width).astype(jnp.bfloat16)
        for part in range(size):
            results[part][index] = field[part]

    plan = dict(
        block=block,
        count=planes,
        line_of=lambda at: lax.rem(lax.div(at, cells_y), cells_x),
        norm=norm,
        put=put,
        order=[],
    )
    shapes = [(planes, cells_x, cells_y, width)] * size
    return attention(
        plan, planes * block, shapes, pieces, gain, w_qkv, w_values, after, "attend_y"
    )


def attend_x(pieces, gain, w_qkv, w_values, after=()):
    size, planes, cells_x, cells_y, width = pieces.shape
    chips = size // 2
    length = size * cells_x
    each = length * cells_y
    together = max(1, min(cells_y, BLOCK // length))
    block = together * length
    columns = [slice(at, at + LANES) for at in range(0, width, LANES)]

    def norm(index, operands, gain, normed, order):
        field = operands[0][:, index].astype(jnp.float32).reshape(each, width)
        field = normalize(field, gain)
        for part, lanes in enumerate(columns):
            order[part] = field[:, lanes]
        for y in range(cells_y):
            at = index * each + y * length
            for part, lanes in enumerate(columns):
                line = order[part, pl.ds(y, length, stride=cells_y), :]
                normed[at : at + length, lanes] = line.astype(jnp.bfloat16)

    def put(index, at, out, results, order):
        for line in range(together):
            rows = slice(line * length, (line + 1) * length)
            for part, lanes in enumerate(columns):
                where = pl.ds(at // length + line, length, stride=cells_y)
                order[part, where, :] = out[rows, lanes]
        if at + block < each:
            return
        device = lax.axis_index("gx")
        chip, core = device // 2, lax.rem(device, 2)
        per = cells_x * cells_y
        for flip in range(chips):
            for which, lane in enumerate((core, 1 - core)):
                start = pl.multiple_of(((chip ^ flip) * 2 + lane) * per, per)
                for part, lanes in enumerate(columns):
                    field = order[part, pl.ds(start, per), :].reshape(cells_x, cells_y, LANES)
                    results[flip][which, index, :, :, lanes] = field.astype(jnp.bfloat16)

    plan = dict(
        block=block,
        count=planes,
        line_of=lambda at: lax.div(at, length),
        norm=norm,
        put=put,
        order=[(width // LANES, each, LANES)],
    )
    shapes = [(2, planes, cells_x, cells_y, width)] * chips
    return attention(
        plan, planes * each, shapes, [pieces], gain, w_qkv, w_values, after, "attend_x"
    )


def pack_kernel(count, *refs):
    out, sems = refs[-2:]
    for copy in start_copies([(refs[at].at[1], out.at[at]) for at in range(count)], sems):
        copy.wait()


def pack(pieces):
    count = len(pieces)
    return pl.pallas_call(
        functools.partial(pack_kernel, count),
        out_shape=jax.ShapeDtypeStruct((count,) + pieces[0].shape[1:], pieces[0].dtype),
        in_specs=[VMEM] * count,
        out_specs=VMEM,
        scratch_shapes=[pltpu.SemaphoreType.DMA((count,))],
        compiler_params=params(),
        cost_estimate=cost(0),
        name="pack_x",
    )(*pieces)


def base_kernel(count, along_time_ref, *refs):
    pieces, sibling, out_ref = refs[:count], refs[count], refs[-1]
    planes = pieces[0].shape[1]
    device = lax.axis_index("gx")
    chip, core = device // 2, lax.rem(device, 2)
    for index in range(count):
        for lane, source in ((core, pieces[index].at[0]), (1 - core, sibling.at[index])):
            at = pl.ds(((chip ^ index) * 2 + lane) * planes, planes)
            out_ref[at] = along_time_ref[at].astype(jnp.float32) + source[...].astype(jnp.float32)


def add_x(along_time, pieces, sibling):
    return pl.pallas_call(
        functools.partial(base_kernel, len(pieces)),
        out_shape=jax.ShapeDtypeStruct(along_time.shape, jnp.float32),
        in_specs=[VMEM] * (2 + len(pieces)),
        out_specs=VMEM,
        compiler_params=params(),
        cost_estimate=cost(0),
        name="add_x",
    )(along_time, *pieces, sibling)


def final_kernel(size, chunk, w_ref, tokens_ref, base_ref, *refs):
    pieces = refs[:size]
    out_ref, held_ref, sems = refs[-3:]
    _, planes, cells_x, cells_y, width = held_ref.shape
    group = tokens_ref.shape[0] // size
    me = lax.axis_index("gy")
    storing = []
    for flip in range(size):
        where = pl.ds((me ^ flip) * group + chunk * planes, planes)
        mixed = base_ref[where] + pieces[flip][...].astype(jnp.float32)
        mixed = mixed.reshape(planes * cells_x * cells_y, width).astype(jnp.bfloat16)
        update = jnp.dot(mixed, w_ref[...], preferred_element_type=jnp.float32)
        field = tokens_ref[where].astype(jnp.float32)
        held_ref[flip] = (field + update.reshape(field.shape)).astype(jnp.bfloat16)
        copy = pltpu.make_async_copy(held_ref.at[flip], out_ref.at[where], sems.at[flip])
        copy.start()
        storing.append(copy)
    for copy in storing:
        copy.wait()


def finish(chunk, w_out, tokens, base, pieces, result):
    size = len(pieces)
    earlier = [] if result is None else [result]
    return pl.pallas_call(
        functools.partial(final_kernel, size, chunk),
        out_shape=jax.ShapeDtypeStruct(tokens.shape, tokens.dtype),
        in_specs=[VMEM] * (3 + size) + [ANY] * len(earlier),
        out_specs=ANY,
        scratch_shapes=[
            pltpu.VMEM((size,) + pieces[0].shape, tokens.dtype),
            pltpu.SemaphoreType.DMA((size,)),
        ],
        input_output_aliases={3 + size: 0} if earlier else {},
        compiler_params=params(),
        cost_estimate=cost(0),
        name="finish",
    )(w_out, tokens, base, *pieces, *earlier)


def cut_kernel(size, planes, tokens_ref, *refs):
    outs, sems = refs[:size], refs[-1]
    me = lax.axis_index("gy")
    pairs = [(tokens_ref.at[pl.ds((me ^ flip) * planes, planes)], outs[flip]) for flip in range(size)]
    for copy in start_copies(pairs, sems):
        copy.wait()


def cut(tokens, size, planes):
    piece = jax.ShapeDtypeStruct((planes,) + tokens.shape[1:], tokens.dtype)
    return pl.pallas_call(
        functools.partial(cut_kernel, size, planes),
        out_shape=[piece] * size,
        in_specs=[ANY],
        out_specs=[HBM] * size,
        scratch_shapes=[pltpu.SemaphoreType.DMA((size,))],
        compiler_params=params(),
        cost_estimate=cost(0),
        name="cut",
    )(tokens)


def trade(pieces, axis="gy", factor=1):
    size = factor * len(pieces)
    return [
        piece
        if flip == 0
        else lax.ppermute(piece, axis, [(at, at ^ (factor * flip)) for at in range(size)])
        for flip, piece in enumerate(pieces)
    ]


def body(count_x, count_y, tokens, norm_gain, w_qkv, w_out):
    batch, steps, cells_x, cells_y, width = tokens.shape
    lines = batch * steps
    plane_shape = (cells_x, cells_y, width)
    gain = norm_gain.reshape(1, width)
    chunks = math.gcd(Y_CHUNKS, lines // count_y)
    chunk_planes = lines // count_y // chunks
    flat = tokens.reshape((lines,) + plane_shape)
    w_values = w_qkv[:, 2 * width :].T

    swap = [(at, at ^ 1) for at in range(count_x)]
    y_pieces = trade(cut(flat, count_y, lines // count_y))
    along_time = attend_time(tokens, gain, w_qkv, w_values)
    x_pieces = lax.all_to_all(
        flat.reshape((count_x, lines // count_x) + plane_shape), "gx", 0, 0, tiled=True
    )
    along_x = attend_x(x_pieces, gain, w_qkv, w_values, [along_time])
    last = along_x[0]
    returned = []
    for chunk in range(chunks):
        out = attend_y(
            y_pieces, chunk * chunk_planes, chunk_planes, gain, w_qkv, w_values, [last]
        )
        last = out[0]
        returned.append(trade(out))
    along_x = trade(along_x, "gx", 2)
    sibling = lax.ppermute(pack(along_x), "gx", swap)
    base = add_x(along_time.reshape((lines,) + plane_shape), along_x, sibling)

    result = None
    for chunk, pieces in enumerate(returned):
        result = finish(chunk, w_out, flat, base, pieces, result)
    return result.reshape(tokens.shape)


def solution(mesh):
    placed = (P(None, None, "gx", "gy", None), P(), P(), P())
    return jax.shard_map(
        functools.partial(body, mesh.shape["gx"], mesh.shape["gy"]),
        mesh=mesh,
        in_specs=placed,
        out_specs=P(None, None, "gx", "gy", None),
        check_vma=False,
    )
```

time: 144 us -> 63.4 us (0.44)
  local copies, waits for them, and re-layouts: 64.7 us -> 6.63 us
  matrix products: 30.6 us -> 0 us
  other arithmetic: 24.1 us -> 0 us
  Pallas kernels: 0 us -> 19.5 us
  waiting for transfers between devices: 2.99 us -> 12.2 us
  starting transfers between devices: 20 us -> 24.3 us
    reshape x9 -> x0, local copies, waits for them, and re-layouts: 31.4 us -> none  [the longest x3 11.7 us: attend(): key_part = triple[..., width:2 * width].reshape(split)]
    dot_general x10 -> x0, matrix products: 30.6 us -> none  [the longest x3 15.1 us: attend(): jnp.einsum(form_scores, queries, key_part, preferred_element_type=jnp.flo...]
    convert_element_type x8 -> x0, local copies, waits for them, and re-layouts: 22.2 us -> none  [the longest x4 12.6 us: attend(): return mixed.reshape(shape[:-1] + (width,)).astype(jnp.bfloat16)]
    pallas_call x0 -> x9, Pallas kernels: none -> 19.5 us  [the longest x4 15.2 us: attention(): pl.pallas_call(functools.partial(attention_kernel, plan), out_shape=[jax....]
    sub x3 -> x0, other arithmetic: 19 us -> none  [attend(): expo = jnp.exp(scores - highest)]
    ppermute x0 -> x13, starting transfers between devices: none -> 19 us  [the longest x12 18.9 us: trade(): lax.ppermute(piece, axis, [(at, at ^ factor * flip) for at in range(size)])]
    all_to_all x4 -> x1, starting transfers between devices: 20 us -> 5.3 us  [body(): lax.all_to_all(flat.reshape((count_x, lines // count_x) + plane_shape), '...]
    ppermute x0 -> x13, waiting for transfers between devices: none -> 9.57 us  [the longest x12 9.57 us: trade(): lax.ppermute(piece, axis, [(at, at ^ factor * flip) for at in range(size)])]
  transfers between devices with their start and end apart: 4 -> 14, of which waited for: 1 -> 5; matrix products, arithmetic and copies ran while one was open for 78% -> 2% of each run, Pallas kernels for 0% -> 29%
where the time goes in v2:
time: 63.4 us; the launch traced here: 63 us
  starting transfers between devices  24.3 us (38%)
  Pallas kernels  19.5 us (31%)
  waiting for transfers between devices  12.2 us (19%)
  local copies, waits for them, and re-layouts  6.63 us (10%)
    ppermute x12, starting transfers between devices, trade(): lax.ppermute(piece, axis, [(at, at ^ factor * flip) for at in range(size)])  18.9 us
    pallas_call x4, Pallas kernels, attention(): pl.pallas_call(functools.partial(attention_kernel, plan), out_shape=[jax....  15.2 us
    ppermute x12, waiting for transfers between devices, trade(): lax.ppermute(piece, axis, [(at, at ^ factor * flip) for at in range(size)])  9.57 us
    unnamed x15, local copies, waits for them, and re-layouts  6.63 us
    all_to_all x1, starting transfers between devices, body(): lax.all_to_all(flat.reshape((count_x, lines // count_x) + plane_shape), '...  5.3 us
    all_to_all x1, waiting for transfers between devices, body(): lax.all_to_all(flat.reshape((count_x, lines // count_x) + plane_shape), '...  2.64 us
    pallas_call x2, Pallas kernels, finish(): pl.pallas_call(functools.partial(final_kernel, size, chunk), out_shape=ja...  2.32 us
  transfers between devices with their start and end apart: 14, of which 5 were waited for; matrix products, arithmetic and copies ran while one was open for 2% of the time, Pallas kernels for 29%

profile of v2, /device:TPU:0, one launch (start us, length us, event | category | flops | bytes accessed | tf_op | source)
XLA Modules:
  0.0 63.0 jit_solution(17153397787174013932)
XLA Ops:
  0.0 0.0 copy-start
  0.0 0.0 slice-start
  0.0 5.3 %all-to-all-start = ((bf16[8,4,4,8,512]{4,3,2,1,0:T(8,128)(2,1)}), bf16[8,4,4,8,512]{4,3,2,1,0:T(8,128)(2,1)S(1)}, u32[]{:S(2)}, u32[]{:S(2)}) async-start(bf16[8,4,4,8,512]{4,3,2,1,0:T(8,128)(2,1)} %bitcast.6), calls=%async_computation | async-start | bytes 2097152 | tf_op jit(solution)/shard_map/all_to_all | solution.py:378
  5.3 0.0 copy-start.6
  5.3 0.0 copy-done
  5.3 0.9 %cut.1 = (bf16[8,4,8,512]{3,2,1,0:T(8,128)(2,1)S(1)}, bf16[8,4,8,512]{3,2,1,0:T(8,128)(2,1)}, bf16[8,4,8,512]{3,2,1,0:T(8,128)(2,1)}, bf16[8,4,8,512]{3,2,1,0:T(8,128)(2,1)}) custom-call(bf16[32,4,8,512]{3,2,1,0:T(8,128)(2,1)S(1)} %bitcast.7), custom_call_target="tpu_custom_call" | custom-call | flops 1000 | bytes 1000 | tf_op jit(solution)/shard_map/cut/pallas_call | solution.py:343
  6.3 1.6 %collective-permute-start.4 = (bf16[8,4,8,512]{3,2,1,0:T(8,128)(2,1)}, bf16[8,4,8,512]{3,2,1,0:T(8,128)(2,1)}, u32[]{:S(2)}, u32[]{:S(2)}) collective-permute-start(bf16[8,4,8,512]{3,2,1,0:T(8,128)(2,1)} %get-tuple-element.26), channel_id=1, source_target_pairs={{0,1},{1,0},{2,3},{3,2},{4,5},{5,4},{6,7},{7,6},{8,9},{9,8},{10,11... | collective-permute-start | bytes 786440 | tf_op jit(solution)/shard_map/ppermute | solution.py:360
  7.9 2.6 %collective-permute-start.5 = (bf16[8,4,8,512]{3,2,1,0:T(8,128)(2,1)}, bf16[8,4,8,512]{3,2,1,0:T(8,128)(2,1)}, u32[]{:S(2)}, u32[]{:S(2)}) collective-permute-start(bf16[8,4,8,512]{3,2,1,0:T(8,128)(2,1)} %get-tuple-element.27), channel_id=1, source_target_pairs={{0,2},{1,3},{2,0},{3,1},{4,6},{5,7},{6,4},{7,5},{8,10},{9,11},{10,... | collective-permute-start | bytes 786440 | tf_op jit(solution)/shard_map/ppermute | solution.py:360
  10.5 0.2 collective-permute-start.6
  10.7 0.0 slice-done
  10.7 1.0 %copy.7 = bf16[512,512]{0,1:T(8,128)(2,1)} copy(bf16[512,512]{1,0:T(8,128)(2,1)S(1)} %slice-done) | data formatting | bytes 1048576
  11.7 0.0 copy-done.6
  11.7 0.0 copy-start.2
  11.7 1.0 %copy-done.2 = bf16[512,512]{0,1:T(8,128)(2,1)S(1)} copy-done((bf16[512,512]{0,1:T(8,128)(2,1)S(1)}, bf16[512,512]{0,1:T(8,128)(2,1)}, u32[]{:S(2)}) %copy-start.2) | copy-done | bytes 524312
  12.8 0.0 copy-start.4
  12.8 1.4 %copy-done.4 = bf16[512,1536]{1,0:T(8,128)(2,1)S(1)} copy-done((bf16[512,1536]{1,0:T(8,128)(2,1)S(1)}, bf16[512,1536]{1,0:T(8,128)(2,1)}, u32[]{:S(2)}) %copy-start.4) | copy-done | bytes 1572888
  14.2 3.9 %attend_time.1.refs_1_ = bf16[2,16,4,8,512]{4,3,2,1,0:T(8,128)(2,1)S(1)} custom-call(f32[1,512]{1,0:T(1,128)S(1)} %bitcast.15, bf16[512,1536]{1,0:T(8,128)(2,1)S(1)} %copy-done.4, bf16[512,512]{1,0:T(8,128)(2,1)S(1)} %bitcast.11, bf16[2,16,4,8,512]{4,3,2,1,0:T(8,128)(2,1)S(1)} %copy-done), custom_call_target="tpu_custom_call" | custom-call | flops 5750001152 | bytes 18451000 | tf_op jit(solution)/shard_map/attend_time/pallas_call | solution.py:122
  18.1 2.6 %all-to-all-done.refs_0_ = bf16[8,4,4,8,512]{4,3,2,1,0:T(8,128)(2,1)S(1)} async-done(((bf16[8,4,4,8,512]{4,3,2,1,0:T(8,128)(2,1)}), bf16[8,4,4,8,512]{4,3,2,1,0:T(8,128)(2,1)S(1)}, u32[]{:S(2)}, u32[]{:S(2)}) %all-to-all-start) | async-done | bytes 1048608 | tf_op jit(solution)/shard_map/all_to_all | solution.py:378
  20.7 0.0 copy-start.3
  20.7 1.0 %copy-done.3 = bf16[512,512]{0,1:T(8,128)(2,1)S(1)} copy-done((bf16[512,512]{0,1:T(8,128)(2,1)S(1)}, bf16[512,512]{0,1:T(8,128)(2,1)}, u32[]{:S(2)}) %copy-start.3) | copy-done | bytes 524312
  21.8 0.0 copy-start.5
  21.8 1.4 %copy-done.5 = bf16[512,1536]{1,0:T(8,128)(2,1)S(1)} copy-done((bf16[512,1536]{1,0:T(8,128)(2,1)S(1)}, bf16[512,1536]{1,0:T(8,128)(2,1)}, u32[]{:S(2)}) %copy-start.5) | copy-done | bytes 1572888
  23.2 4.3 %attend_x.1 = (bf16[2,4,4,8,512]{4,3,2,1,0:T(8,128)(2,1)S(1)}, bf16[2,4,4,8,512]{4,3,2,1,0:T(8,128)(2,1)S(1)}, bf16[2,4,4,8,512]{4,3,2,1,0:T(8,128)(2,1)S(1)}, bf16[2,4,4,8,512]{4,3,2,1,0:T(8,128)(2,1)S(1)}) custom-call(f32[1,512]{1,0:T(1,128)S(1)} %bitcast.16, bf16[512,1536]{1,0:T(8,128)(2,1)S(1)} %copy-done.5, bf16[512,512]{1,0:T(8,128)(2,1)S(1)} %bitcast.12, ...), custom_call_target="tpu_custom_call" | custom-call | flops 5750001152 | bytes 18451000 | tf_op jit(solution)/shard_map/attend_x/pallas_call | solution.py:122
  27.5 0.6 collective-permute-start
  28.1 0.6 %collective-permute-start.1 = (bf16[2,4,4,8,512]{4,3,2,1,0:T(8,128)(2,1)S(1)}, bf16[2,4,4,8,512]{4,3,2,1,0:T(8,128)(2,1)S(1)}, u32[]{:S(2)}, u32[]{:S(2)}) collective-permute-start(bf16[2,4,4,8,512]{4,3,2,1,0:T(8,128)(2,1)S(1)} %get-tuple-element.23), channel_id=1, source_target_pairs={{0,16},{4,20},{8,24},{12,28},{16,0},{20,4},{24,8},{28,12},{1,17},{... | collective-permute-start | bytes 786440 | tf_op jit(solution)/shard_map/ppermute | solution.py:360
  28.7 0.0 collective-permute-done.4.refs_1_
  28.8 2.3 %collective-permute-start.2 = (bf16[2,4,4,8,512]{4,3,2,1,0:T(8,128)(2,1)S(1)}, bf16[2,4,4,8,512]{4,3,2,1,0:T(8,128)(2,1)S(1)}, u32[]{:S(2)}, u32[]{:S(2)}) collective-permute-start(bf16[2,4,4,8,512]{4,3,2,1,0:T(8,128)(2,1)S(1)} %get-tuple-element.24), channel_id=1, source_target_pairs={{0,24},{4,28},{8,16},{12,20},{16,8},{20,12},{24,0},{28,4},{1,25},{... | collective-permute-start | bytes 786440 | tf_op jit(solution)/shard_map/ppermute | solution.py:360
  31.1 0.0 collective-permute-done.5.refs_2_
  31.1 0.0 collective-permute-done.6.refs_3_
  31.1 3.5 %attend_y.2 = (bf16[4,4,8,512]{3,2,1,0:T(8,128)(2,1)S(1)}, bf16[4,4,8,512]{3,2,1,0:T(8,128)(2,1)S(1)}, bf16[4,4,8,512]{3,2,1,0:T(8,128)(2,1)S(1)}, bf16[4,4,8,512]{3,2,1,0:T(8,128)(2,1)S(1)}) custom-call(f32[1,512]{1,0:T(1,128)S(1)} %bitcast.17, bf16[512,1536]{1,0:T(8,128)(2,1)S(1)} %copy-done.5, bf16[512,512]{1,0:T(8,128)(2,1)S(1)} %bitcast.13, ...), custom_call_target="tpu_custom_call" | custom-call | flops 5750001152 | bytes 18451000 | tf_op jit(solution)/shard_map/attend_y/pallas_call | solution.py:122
  34.5 4.0 %collective-permute-start.10 = (bf16[4,4,8,512]{3,2,1,0:T(8,128)(2,1)S(1)}, bf16[4,4,8,512]{3,2,1,0:T(8,128)(2,1)S(1)}, u32[]{:S(2)}, u32[]{:S(2)}) collective-permute-start(bf16[4,4,8,512]{3,2,1,0:T(8,128)(2,1)S(1)} %get-tuple-element.34), channel_id=1, source_target_pairs={{0,1},{1,0},{2,3},{3,2},{4,5},{5,4},{6,7},{7,6},{8,9},{9,8},{10,11... | collective-permute-start | bytes 393224 | tf_op jit(solution)/shard_map/ppermute | solution.py:360
  38.6 1.1 %collective-permute-start.11 = (bf16[4,4,8,512]{3,2,1,0:T(8,128)(2,1)S(1)}, bf16[4,4,8,512]{3,2,1,0:T(8,128)(2,1)S(1)}, u32[]{:S(2)}, u32[]{:S(2)}) collective-permute-start(bf16[4,4,8,512]{3,2,1,0:T(8,128)(2,1)S(1)} %get-tuple-element.35), channel_id=1, source_target_pairs={{0,2},{1,3},{2,0},{3,1},{4,6},{5,7},{6,4},{7,5},{8,10},{9,11},{10,... | collective-permute-start | bytes 393224 | tf_op jit(solution)/shard_map/ppermute | solution.py:360
  39.6 0.0 collective-permute-done.refs_1_
  39.6 1.4 %collective-permute-start.12 = (bf16[4,4,8,512]{3,2,1,0:T(8,128)(2,1)S(1)}, bf16[4,4,8,512]{3,2,1,0:T(8,128)(2,1)S(1)}, u32[]{:S(2)}, u32[]{:S(2)}) collective-permute-start(bf16[4,4,8,512]{3,2,1,0:T(8,128)(2,1)S(1)} %get-tuple-element.36), channel_id=1, source_target_pairs={{0,3},{1,2},{2,1},{3,0},{4,7},{5,6},{6,5},{7,4},{8,11},{9,10},{10,... | collective-permute-start | bytes 393224 | tf_op jit(solution)/shard_map/ppermute | solution.py:360
  41.0 0.8 %collective-permute-done.1.refs_2_ = bf16[2,4,4,8,512]{4,3,2,1,0:T(8,128)(2,1)S(1)} collective-permute-done((bf16[2,4,4,8,512]{4,3,2,1,0:T(8,128)(2,1)S(1)}, bf16[2,4,4,8,512]{4,3,2,1,0:T(8,128)(2,1)S(1)}, u32[]{:S(2)}, u32[]{:S(2)}) %collective-permute-start.1) | collective-permute-done | bytes 262176 | tf_op jit(solution)/shard_map/ppermute | solution.py:360
  41.8 0.0 collective-permute-done.2.refs_3_
  41.8 0.9 %pack_x.1 = bf16[4,4,4,8,512]{4,3,2,1,0:T(8,128)(2,1)S(1)} custom-call(bf16[2,4,4,8,512]{4,3,2,1,0:T(8,128)(2,1)S(1)} %get-tuple-element.21.refs_0_.refs_4_, bf16[2,4,4,8,512]{4,3,2,1,0:T(8,128)(2,1)S(1)} %collective-permute-done.refs_1_, bf16[2,4,4,8,512]{4,3,2,1,0:T(8,128)(2,1)S(1)} %collective-permute-done.1.refs_2_, ...), custom_call_target="tpu_custom_call" | custom-call | flops 1000 | bytes 1000 | tf_op jit(solution)/shard_map/pack_x/pallas_call | solution.py:258
  42.7 0.1 collective-permute-start.3
  42.8 3.5 %attend_y.3 = (bf16[4,4,8,512]{3,2,1,0:T(8,128)(2,1)S(1)}, bf16[4,4,8,512]{3,2,1,0:T(8,128)(2,1)S(1)}, bf16[4,4,8,512]{3,2,1,0:T(8,128)(2,1)S(1)}, bf16[4,4,8,512]{3,2,1,0:T(8,128)(2,1)S(1)}) custom-call(f32[1,512]{1,0:T(1,128)S(1)} %bitcast.18, bf16[512,1536]{1,0:T(8,128)(2,1)S(1)} %copy-done.5, bf16[512,512]{1,0:T(8,128)(2,1)S(1)} %bitcast.14, ...), custom_call_target="tpu_custom_call" | custom-call | flops 5750001152 | bytes 18451000 | tf_op jit(solution)/shard_map/attend_y/pallas_call | solution.py:122
  46.3 1.6 %collective-permute-start.7 = (bf16[4,4,8,512]{3,2,1,0:T(8,128)(2,1)S(1)}, bf16[4,4,8,512]{3,2,1,0:T(8,128)(2,1)S(1)}, u32[]{:S(2)}, u32[]{:S(2)}) collective-permute-start(bf16[4,4,8,512]{3,2,1,0:T(8,128)(2,1)S(1)} %get-tuple-element.31), channel_id=1, source_target_pairs={{0,1},{1,0},{2,3},{3,2},{4,5},{5,4},{6,7},{7,6},{8,9},{9,8},{10,11... | collective-permute-start | bytes 393224 | tf_op jit(solution)/shard_map/ppermute | solution.py:360
  47.9 0.0 collective-permute-done.10.refs_1_
  47.9 2.6 %collective-permute-start.8 = (bf16[4,4,8,512]{3,2,1,0:T(8,128)(2,1)S(1)}, bf16[4,4,8,512]{3,2,1,0:T(8,128)(2,1)S(1)}, u32[]{:S(2)}, u32[]{:S(2)}) collective-permute-start(bf16[4,4,8,512]{3,2,1,0:T(8,128)(2,1)S(1)} %get-tuple-element.32), channel_id=1, source_target_pairs={{0,2},{1,3},{2,0},{3,1},{4,6},{5,7},{6,4},{7,5},{8,10},{9,11},{10,... | collective-permute-start | bytes 393224 | tf_op jit(solution)/shard_map/ppermute | solution.py:360
  50.5 0.0 collective-permute-done.3.refs_4_
  50.5 0.2 collective-permute-start.9
  50.7 0.0 copy-start.1
  50.7 0.2 add_x.1.base_ref
  51.0 0.1 collective-permute-done.11.refs_2_
  51.0 0.0 collective-permute-done.12.refs_3_
  51.0 0.7 %copy-done.1 = bf16[512,512]{1,0:T(8,128)(2,1)S(1)} copy-done((bf16[512,512]{1,0:T(8,128)(2,1)S(1)}, bf16[512,512]{1,0:T(8,128)(2,1)}, u32[]{:S(2)}) %copy-start.1) | copy-done | bytes 524312
  51.8 1.2 %finish.2.refs_4_ = bf16[32,4,8,512]{3,2,1,0:T(8,128)(2,1)} custom-call(bf16[512,512]{1,0:T(8,128)(2,1)S(1)} %copy-done.1, bf16[32,4,8,512]{3,2,1,0:T(8,128)(2,1)S(1)} %bitcast.8, f32[32,4,8,512]{3,2,1,0:T(8,128)S(1)} %add_x.1.base_ref, bf16[4,4,8,512]{3,2,1,0:T(8,128)(2,1)S(1)} %get-tuple-element.29.refs_4_.refs_0_, ...), custom_call_target="tpu_custom_call" | custom-call | flops 1000 | bytes 1000 | tf_op jit(solution)/shard_map/finish/pallas_call | solution.py:317
  52.9 2.0 %collective-permute-done.7.refs_1_ = bf16[4,4,8,512]{3,2,1,0:T(8,128)(2,1)S(1)} collective-permute-done((bf16[4,4,8,512]{3,2,1,0:T(8,128)(2,1)S(1)}, bf16[4,4,8,512]{3,2,1,0:T(8,128)(2,1)S(1)}, u32[]{:S(2)}, u32[]{:S(2)}) %collective-permute-start.7) | collective-permute-done | bytes 131104 | tf_op jit(solution)/shard_map/ppermute | solution.py:360
  55.0 6.7 %collective-permute-done.8.refs_2_ = bf16[4,4,8,512]{3,2,1,0:T(8,128)(2,1)S(1)} collective-permute-done((bf16[4,4,8,512]{3,2,1,0:T(8,128)(2,1)S(1)}, bf16[4,4,8,512]{3,2,1,0:T(8,128)(2,1)S(1)}, u32[]{:S(2)}, u32[]{:S(2)}) %collective-permute-start.8) | collective-permute-done | bytes 131104 | tf_op jit(solution)/shard_map/ppermute | solution.py:360
  61.6 0.0 collective-permute-done.9.refs_3_
  61.6 1.2 %finish.3 = bf16[32,4,8,512]{3,2,1,0:T(8,128)(2,1)} custom-call(bf16[512,512]{1,0:T(8,128)(2,1)S(1)} %copy-done.1, bf16[32,4,8,512]{3,2,1,0:T(8,128)(2,1)S(1)} %bitcast.9, f32[32,4,8,512]{3,2,1,0:T(8,128)S(1)} %add_x.1.base_ref, bf16[4,4,8,512]{3,2,1,0:T(8,128)(2,1)S(1)} %get-tuple-element.30.refs_0_, ...), custom_call_target="tpu_custom_call", output_to_operand_aliasing={{}: (7, {})} | custom-call | flops 1000 | bytes 1000 | tf_op jit(solution)/shard_map/finish/pallas_call | solution.py:317
Async XLA Ops:
  0.0 5.3 %copy-start = (bf16[2,16,4,8,512]{4,3,2,1,0:T(8,128)(2,1)S(1)}, bf16[2,16,4,8,512]{4,3,2,1,0:T(8,128)(2,1)}, u32[]{:S(2)}) copy-start(bf16[2,16,4,8,512]{4,3,2,1,0:T(8,128)(2,1)} %refs_0_.1) | copy-start | bytes 3145732
  0.0 10.7 %slice-start = ((bf16[512,1536]{1,0:T(8,128)(2,1)}), bf16[512,512]{1,0:T(8,128)(2,1)S(1)}, s32[]{:S(2)}) async-start(bf16[512,1536]{1,0:T(8,128)(2,1)} %w_ref.9), calls=%async_computation.1 | async-start | bytes 1048576 | tf_op jit(solution)/shard_map/slice | solution.py:373
  0.0 20.7 %all-to-all-start = ((bf16[8,4,4,8,512]{4,3,2,1,0:T(8,128)(2,1)}), bf16[8,4,4,8,512]{4,3,2,1,0:T(8,128)(2,1)S(1)}, u32[]{:S(2)}, u32[]{:S(2)}) async-start(bf16[8,4,4,8,512]{4,3,2,1,0:T(8,128)(2,1)} %bitcast.6), calls=%async_computation | async-start | bytes 2097152 | tf_op jit(solution)/shard_map/all_to_all | solution.py:378
  5.3 6.4 %copy-start.6 = (f32[512]{0:T(512)S(1)}, f32[512]{0:T(512)}, u32[]{:S(2)}) copy-start(f32[512]{0:T(512)} %param.5) | copy-start | bytes 6148
  6.3 22.5 %collective-permute-start.4 = (bf16[8,4,8,512]{3,2,1,0:T(8,128)(2,1)}, bf16[8,4,8,512]{3,2,1,0:T(8,128)(2,1)}, u32[]{:S(2)}, u32[]{:S(2)}) collective-permute-start(bf16[8,4,8,512]{3,2,1,0:T(8,128)(2,1)} %get-tuple-element.26), channel_id=1, source_target_pairs={{0,1},{1,0},{2,3},{3,2},{4,5},{5,4},{6,7},{7,6},{8,9},{9,8},{10,11... | collective-permute-start | bytes 786440 | tf_op jit(solution)/shard_map/ppermute | solution.py:360
  7.9 23.1 %collective-permute-start.5 = (bf16[8,4,8,512]{3,2,1,0:T(8,128)(2,1)}, bf16[8,4,8,512]{3,2,1,0:T(8,128)(2,1)}, u32[]{:S(2)}, u32[]{:S(2)}) collective-permute-start(bf16[8,4,8,512]{3,2,1,0:T(8,128)(2,1)} %get-tuple-element.27), channel_id=1, source_target_pairs={{0,2},{1,3},{2,0},{3,1},{4,6},{5,7},{6,4},{7,5},{8,10},{9,11},{10,... | collective-permute-start | bytes 786440 | tf_op jit(solution)/shard_map/ppermute | solution.py:360
  10.5 20.6 %collective-permute-start.6 = (bf16[8,4,8,512]{3,2,1,0:T(8,128)(2,1)}, bf16[8,4,8,512]{3,2,1,0:T(8,128)(2,1)}, u32[]{:S(2)}, u32[]{:S(2)}) collective-permute-start(bf16[8,4,8,512]{3,2,1,0:T(8,128)(2,1)} %get-tuple-element.28), channel_id=1, source_target_pairs={{0,3},{1,2},{2,1},{3,0},{4,7},{5,6},{6,5},{7,4},{8,11},{9,10},{10,... | collective-permute-start | bytes 786440 | tf_op jit(solution)/shard_map/ppermute | solution.py:360
  11.7 1.0 %copy-start.2 = (bf16[512,512]{0,1:T(8,128)(2,1)S(1)}, bf16[512,512]{0,1:T(8,128)(2,1)}, u32[]{:S(2)}) copy-start(bf16[512,512]{0,1:T(8,128)(2,1)} %copy.7) | copy-start | bytes 1572868
  12.8 1.4 %copy-start.4 = (bf16[512,1536]{1,0:T(8,128)(2,1)S(1)}, bf16[512,1536]{1,0:T(8,128)(2,1)}, u32[]{:S(2)}) copy-start(bf16[512,1536]{1,0:T(8,128)(2,1)} %w_ref.9) | copy-start | bytes 4718596
  20.7 1.0 %copy-start.3 = (bf16[512,512]{0,1:T(8,128)(2,1)S(1)}, bf16[512,512]{0,1:T(8,128)(2,1)}, u32[]{:S(2)}) copy-start(bf16[512,512]{0,1:T(8,128)(2,1)} %copy.7) | copy-start | bytes 1572868
  21.8 1.4 %copy-start.5 = (bf16[512,1536]{1,0:T(8,128)(2,1)S(1)}, bf16[512,1536]{1,0:T(8,128)(2,1)}, u32[]{:S(2)}) copy-start(bf16[512,1536]{1,0:T(8,128)(2,1)} %w_ref.9) | copy-start | bytes 4718596
  27.5 12.1 %collective-permute-start = (bf16[2,4,4,8,512]{4,3,2,1,0:T(8,128)(2,1)S(1)}, bf16[2,4,4,8,512]{4,3,2,1,0:T(8,128)(2,1)S(1)}, u32[]{:S(2)}, u32[]{:S(2)}) collective-permute-start(bf16[2,4,4,8,512]{4,3,2,1,0:T(8,128)(2,1)S(1)} %get-tuple-element.22), channel_id=1, source_target_pairs={{0,8},{4,12},{8,0},{12,4},{16,24},{20,28},{24,16},{28,20},{1,9},{5... | collective-permute-start | bytes 786440 | tf_op jit(solution)/shard_map/ppermute | solution.py:360
  28.1 13.7 %collective-permute-start.1 = (bf16[2,4,4,8,512]{4,3,2,1,0:T(8,128)(2,1)S(1)}, bf16[2,4,4,8,512]{4,3,2,1,0:T(8,128)(2,1)S(1)}, u32[]{:S(2)}, u32[]{:S(2)}) collective-permute-start(bf16[2,4,4,8,512]{4,3,2,1,0:T(8,128)(2,1)S(1)} %get-tuple-element.23), channel_id=1, source_target_pairs={{0,16},{4,20},{8,24},{12,28},{16,0},{20,4},{24,8},{28,12},{1,17},{... | collective-permute-start | bytes 786440 | tf_op jit(solution)/shard_map/ppermute | solution.py:360
  28.8 13.1 %collective-permute-start.2 = (bf16[2,4,4,8,512]{4,3,2,1,0:T(8,128)(2,1)S(1)}, bf16[2,4,4,8,512]{4,3,2,1,0:T(8,128)(2,1)S(1)}, u32[]{:S(2)}, u32[]{:S(2)}) collective-permute-start(bf16[2,4,4,8,512]{4,3,2,1,0:T(8,128)(2,1)S(1)} %get-tuple-element.24), channel_id=1, source_target_pairs={{0,24},{4,28},{8,16},{12,20},{16,8},{20,12},{24,0},{28,4},{1,25},{... | collective-permute-start | bytes 786440 | tf_op jit(solution)/shard_map/ppermute | solution.py:360
  34.5 13.4 %collective-permute-start.10 = (bf16[4,4,8,512]{3,2,1,0:T(8,128)(2,1)S(1)}, bf16[4,4,8,512]{3,2,1,0:T(8,128)(2,1)S(1)}, u32[]{:S(2)}, u32[]{:S(2)}) collective-permute-start(bf16[4,4,8,512]{3,2,1,0:T(8,128)(2,1)S(1)} %get-tuple-element.34), channel_id=1, source_target_pairs={{0,1},{1,0},{2,3},{3,2},{4,5},{5,4},{6,7},{7,6},{8,9},{9,8},{10,11... | collective-permute-start | bytes 393224 | tf_op jit(solution)/shard_map/ppermute | solution.py:360
  38.6 12.5 %collective-permute-start.11 = (bf16[4,4,8,512]{3,2,1,0:T(8,128)(2,1)S(1)}, bf16[4,4,8,512]{3,2,1,0:T(8,128)(2,1)S(1)}, u32[]{:S(2)}, u32[]{:S(2)}) collective-permute-start(bf16[4,4,8,512]{3,2,1,0:T(8,128)(2,1)S(1)} %get-tuple-element.35), channel_id=1, source_target_pairs={{0,2},{1,3},{2,0},{3,1},{4,6},{5,7},{6,4},{7,5},{8,10},{9,11},{10,... | collective-permute-start | bytes 393224 | tf_op jit(solution)/shard_map/ppermute | solution.py:360
  39.6 11.4 %collective-permute-start.12 = (bf16[4,4,8,512]{3,2,1,0:T(8,128)(2,1)S(1)}, bf16[4,4,8,512]{3,2,1,0:T(8,128)(2,1)S(1)}, u32[]{:S(2)}, u32[]{:S(2)}) collective-permute-start(bf16[4,4,8,512]{3,2,1,0:T(8,128)(2,1)S(1)} %get-tuple-element.36), channel_id=1, source_target_pairs={{0,3},{1,2},{2,1},{3,0},{4,7},{5,6},{6,5},{7,4},{8,11},{9,10},{10,... | collective-permute-start | bytes 393224 | tf_op jit(solution)/shard_map/ppermute | solution.py:360
  42.7 7.8 %collective-permute-start.3 = (bf16[4,4,4,8,512]{4,3,2,1,0:T(8,128)(2,1)S(1)}, bf16[4,4,4,8,512]{4,3,2,1,0:T(8,128)(2,1)S(1)}, u32[]{:S(2)}, u32[]{:S(2)}) collective-permute-start(bf16[4,4,4,8,512]{4,3,2,1,0:T(8,128)(2,1)S(1)} %pack_x.1), channel_id=1, source_target_pairs={{0,4},{4,0},{8,12},{12,8},{16,20},{20,16},{24,28},{28,24},{1,5},{5... | collective-permute-start | bytes 1572872 | tf_op jit(solution)/shard_map/ppermute | solution.py:391
  46.3 8.7 %collective-permute-start.7 = (bf16[4,4,8,512]{3,2,1,0:T(8,128)(2,1)S(1)}, bf16[4,4,8,512]{3,2,1,0:T(8,128)(2,1)S(1)}, u32[]{:S(2)}, u32[]{:S(2)}) collective-permute-start(bf16[4,4,8,512]{3,2,1,0:T(8,128)(2,1)S(1)} %get-tuple-element.31), channel_id=1, source_target_pairs={{0,1},{1,0},{2,3},{3,2},{4,5},{5,4},{6,7},{7,6},{8,9},{9,8},{10,11... | collective-permute-start | bytes 393224 | tf_op jit(solution)/shard_map/ppermute | solution.py:360
  47.9 13.7 %collective-permute-start.8 = (bf16[4,4,8,512]{3,2,1,0:T(8,128)(2,1)S(1)}, bf16[4,4,8,512]{3,2,1,0:T(8,128)(2,1)S(1)}, u32[]{:S(2)}, u32[]{:S(2)}) collective-permute-start(bf16[4,4,8,512]{3,2,1,0:T(8,128)(2,1)S(1)} %get-tuple-element.32), channel_id=1, source_target_pairs={{0,2},{1,3},{2,0},{3,1},{4,6},{5,7},{6,4},{7,5},{8,10},{9,11},{10,... | collective-permute-start | bytes 393224 | tf_op jit(solution)/shard_map/ppermute | solution.py:360
  50.5 11.1 %collective-permute-start.9 = (bf16[4,4,8,512]{3,2,1,0:T(8,128)(2,1)S(1)}, bf16[4,4,8,512]{3,2,1,0:T(8,128)(2,1)S(1)}, u32[]{:S(2)}, u32[]{:S(2)}) collective-permute-start(bf16[4,4,8,512]{3,2,1,0:T(8,128)(2,1)S(1)} %get-tuple-element.33), channel_id=1, source_target_pairs={{0,3},{1,2},{2,1},{3,0},{4,7},{5,6},{6,5},{7,4},{8,11},{9,10},{10,... | collective-permute-start | bytes 393224 | tf_op jit(solution)/shard_map/ppermute | solution.py:360
  50.7 1.0 %copy-start.1 = (bf16[512,512]{1,0:T(8,128)(2,1)S(1)}, bf16[512,512]{1,0:T(8,128)(2,1)}, u32[]{:S(2)}) copy-start(bf16[512,512]{1,0:T(8,128)(2,1)} %w_ref.11) | copy-start | bytes 1572868

commit v3 on v2

--- a/solution.py
+++ b/solution.py
@@ -290,58 +290,61 @@
     )(along_time, *pieces, sibling)
 
 
-def final_kernel(size, chunk, w_ref, tokens_ref, base_ref, *refs):
-    pieces = refs[:size]
+def final_kernel(size, flips, first, w_ref, tokens_ref, base_ref, *refs):
+    pieces = refs[: len(flips)]
     out_ref, held_ref, sems = refs[-3:]
     _, planes, cells_x, cells_y, width = held_ref.shape
     group = tokens_ref.shape[0] // size
     me = lax.axis_index("gy")
     storing = []
-    for flip in range(size):
-        where = pl.ds((me ^ flip) * group + chunk * planes, planes)
-        mixed = base_ref[where] + pieces[flip][...].astype(jnp.float32)
+    for at, flip in enumerate(flips):
+        where = pl.ds((me ^ flip) * group + first, planes)
+        mixed = base_ref[where] + pieces[at][...].astype(jnp.float32)
         mixed = mixed.reshape(planes * cells_x * cells_y, width).astype(jnp.bfloat16)
         update = jnp.dot(mixed, w_ref[...], preferred_element_type=jnp.float32)
         field = tokens_ref[where].astype(jnp.float32)
-        held_ref[flip] = (field + update.reshape(field.shape)).astype(jnp.bfloat16)
-        copy = pltpu.make_async_copy(held_ref.at[flip], out_ref.at[where], sems.at[flip])
+        held_ref[at] = (field + update.reshape(field.shape)).astype(jnp.bfloat16)
+        copy = pltpu.make_async_copy(held_ref.at[at], out_ref.at[where], sems.at[at])
         copy.start()
         storing.append(copy)
     for copy in storing:
         copy.wait()
 
 
-def finish(chunk, w_out, tokens, base, pieces, result):
-    size = len(pieces)
+def finish(size, flips, first, w_out, tokens, base, pieces, result):
+    count = len(flips)
     earlier = [] if result is None else [result]
     return pl.pallas_call(
-        functools.partial(final_kernel, size, chunk),
+        functools.partial(final_kernel, size, flips, first),
         out_shape=jax.ShapeDtypeStruct(tokens.shape, tokens.dtype),
-        in_specs=[VMEM] * (3 + size) + [ANY] * len(earlier),
+        in_specs=[VMEM] * (3 + count) + [ANY] * len(earlier),
         out_specs=ANY,
         scratch_shapes=[
-            pltpu.VMEM((size,) + pieces[0].shape, tokens.dtype),
-            pltpu.SemaphoreType.DMA((size,)),
+            pltpu.VMEM((count,) + pieces[0].shape, tokens.dtype),
+            pltpu.SemaphoreType.DMA((count,)),
         ],
-        input_output_aliases={3 + size: 0} if earlier else {},
+        input_output_aliases={3 + count: 0} if earlier else {},
         compiler_params=params(),
         cost_estimate=cost(0),
         name="finish",
     )(w_out, tokens, base, *pieces, *earlier)
 
 
-def cut_kernel(size, planes, tokens_ref, *refs):
-    outs, sems = refs[:size], refs[-1]
+def cut_kernel(flips, planes, tokens_ref, *refs):
+    outs, sems = refs[:-1], refs[-1]
     me = lax.axis_index("gy")
-    pairs = [(tokens_ref.at[pl.ds((me ^ flip) * planes, planes)], outs[flip]) for flip in range(size)]
+    pairs = [
+        (tokens_ref.at[pl.ds((me ^ flip) * planes, planes)], out) for flip, out in zip(flips, outs)
+    ]
     for copy in start_copies(pairs, sems):
         copy.wait()
 
 
-def cut(tokens, size, planes):
+def cut(tokens, flips, planes):
+    size = len(flips)
     piece = jax.ShapeDtypeStruct((planes,) + tokens.shape[1:], tokens.dtype)
     return pl.pallas_call(
-        functools.partial(cut_kernel, size, planes),
+        functools.partial(cut_kernel, flips, planes),
         out_shape=[piece] * size,
         in_specs=[ANY],
         out_specs=[HBM] * size,
@@ -352,13 +355,13 @@
     )(tokens)
 
 
-def trade(pieces, axis="gy", factor=1):
+def trade(pieces, flips, axis="gy", factor=1):
     size = factor * len(pieces)
     return [
         piece
         if flip == 0
         else lax.ppermute(piece, axis, [(at, at ^ (factor * flip)) for at in range(size)])
-        for flip, piece in enumerate(pieces)
+        for flip, piece in zip(flips, pieces)
     ]
 
 
@@ -373,7 +376,8 @@
     w_values = w_qkv[:, 2 * width :].T
 
     swap = [(at, at ^ 1) for at in range(count_x)]
-    y_pieces = trade(cut(flat, count_y, lines // count_y))
+    flips = range(count_y)
+    y_pieces = trade(cut(flat, flips, lines // count_y), flips)
     along_time = attend_time(tokens, gain, w_qkv, w_values)
     x_pieces = lax.all_to_all(
         flat.reshape((count_x, lines // count_x) + plane_shape), "gx", 0, 0, tiled=True
@@ -386,14 +390,27 @@
             y_pieces, chunk * chunk_planes, chunk_planes, gain, w_qkv, w_values, [last]
         )
         last = out[0]
-        returned.append(trade(out))
-    along_x = trade(along_x, "gx", 2)
+        returned.append(dict(zip(flips, trade(out, flips))))
+    along_x = trade(along_x, range(count_x // 2), "gx", 2)
     sibling = lax.ppermute(pack(along_x), "gx", swap)
     base = add_x(along_time.reshape((lines,) + plane_shape), along_x, sibling)
 
     result = None
     for chunk, pieces in enumerate(returned):
-        result = finish(chunk, w_out, flat, base, pieces, result)
+        near = [*range(count_y // 2)]
+        far = [*range(count_y // 2, count_y)]
+        for some in [near, far] if chunk == chunks - 1 else [[0, *range(count_y - 1, 0, -1)]]:
+            if some:
+                result = finish(
+                    count_y,
+                    some,
+                    chunk * chunk_planes,
+                    w_out,
+                    flat,
+                    base,
+                    [pieces[flip] for flip in some],
+                    result,
+                )
     return result.reshape(tokens.shape)
 
 

time: 63.4 us -> 62.4 us (0.984)
  waiting for transfers between devices: 12.2 us -> 11.2 us
  starting transfers between devices: 24.3 us -> 23.4 us
  Pallas kernels: 19.5 us -> 20.4 us
    ppermute x12, waiting for transfers between devices: 9.57 us -> 8.56 us  [trade(): lax.ppermute(piece, axis, [(at, at ^ factor * flip) for at in range(size)])]
    ppermute x12, starting transfers between devices: 18.9 us -> 18 us  [trade(): lax.ppermute(piece, axis, [(at, at ^ factor * flip) for at in range(size)])]
    pallas_call x3 -> x4, Pallas kernels: 3.27 us -> 4.09 us  [the longest x3 3.14 us: finish(): pl.pallas_call(functools.partial(final_kernel, size, flips, first), out_s...]
  transfers between devices with their start and end apart: 14 -> 14, of which waited for: 5 -> 4; matrix products, arithmetic and copies ran while one was open for 2% -> 2% of each run, Pallas kernels for 29% -> 31%
where the time goes in v3:
time: 62.4 us; the launch traced here: 61.9 us
  starting transfers between devices  23.4 us (38%)
  Pallas kernels  20.4 us (33%)
  waiting for transfers between devices  11.2 us (18%)
  local copies, waits for them, and re-layouts  6.69 us (11%)
    ppermute x12, starting transfers between devices, trade(): lax.ppermute(piece, axis, [(at, at ^ factor * flip) for at in range(size)])  18 us
    pallas_call x4, Pallas kernels, attention(): pl.pallas_call(functools.partial(attention_kernel, plan), out_shape=[jax....  15.2 us
    ppermute x12, waiting for transfers between devices, trade(): lax.ppermute(piece, axis, [(at, at ^ factor * flip) for at in range(size)])  8.56 us
    unnamed x15, local copies, waits for them, and re-layouts  6.68 us
    all_to_all x1, starting transfers between devices, body(): lax.all_to_all(flat.reshape((count_x, lines // count_x) + plane_shape), '...  5.3 us
    pallas_call x3, Pallas kernels, finish(): pl.pallas_call(functools.partial(final_kernel, size, flips, first), out_s...  3.14 us
    all_to_all x1, waiting for transfers between devices, body(): lax.all_to_all(flat.reshape((count_x, lines // count_x) + plane_shape), '...  2.64 us
  transfers between devices with their start and end apart: 14, of which 4 were waited for; matrix products, arithmetic and copies ran while one was open for 2% of the time, Pallas kernels for 31%

profile of v3, /device:TPU:0, one launch (start us, length us, event | category | flops | bytes accessed | tf_op | source)
XLA Modules:
  0.0 61.9 jit_solution(16630032853471091901)
XLA Ops:
  0.0 0.0 copy-start
  0.0 0.0 slice-start
  0.0 5.3 %all-to-all-start = ((bf16[8,4,4,8,512]{4,3,2,1,0:T(8,128)(2,1)}), bf16[8,4,4,8,512]{4,3,2,1,0:T(8,128)(2,1)S(1)}, u32[]{:S(2)}, u32[]{:S(2)}) async-start(bf16[8,4,4,8,512]{4,3,2,1,0:T(8,128)(2,1)} %bitcast.6), calls=%async_computation | async-start | bytes 2097152 | tf_op jit(solution)/shard_map/all_to_all | solution.py:382
  5.3 0.0 copy-start.6
  5.3 0.0 copy-done
  5.3 0.9 %cut.1 = (bf16[8,4,8,512]{3,2,1,0:T(8,128)(2,1)S(1)}, bf16[8,4,8,512]{3,2,1,0:T(8,128)(2,1)}, bf16[8,4,8,512]{3,2,1,0:T(8,128)(2,1)}, bf16[8,4,8,512]{3,2,1,0:T(8,128)(2,1)}) custom-call(bf16[32,4,8,512]{3,2,1,0:T(8,128)(2,1)S(1)} %bitcast.7), custom_call_target="tpu_custom_call" | custom-call | flops 1000 | bytes 1000 | tf_op jit(solution)/shard_map/cut/pallas_call | solution.py:346
  6.3 1.6 %collective-permute-start.4 = (bf16[8,4,8,512]{3,2,1,0:T(8,128)(2,1)}, bf16[8,4,8,512]{3,2,1,0:T(8,128)(2,1)}, u32[]{:S(2)}, u32[]{:S(2)}) collective-permute-start(bf16[8,4,8,512]{3,2,1,0:T(8,128)(2,1)} %get-tuple-element.26), channel_id=1, source_target_pairs={{0,1},{1,0},{2,3},{3,2},{4,5},{5,4},{6,7},{7,6},{8,9},{9,8},{10,11... | collective-permute-start | bytes 786440 | tf_op jit(solution)/shard_map/ppermute | solution.py:363
  7.9 2.6 %collective-permute-start.5 = (bf16[8,4,8,512]{3,2,1,0:T(8,128)(2,1)}, bf16[8,4,8,512]{3,2,1,0:T(8,128)(2,1)}, u32[]{:S(2)}, u32[]{:S(2)}) collective-permute-start(bf16[8,4,8,512]{3,2,1,0:T(8,128)(2,1)} %get-tuple-element.27), channel_id=1, source_target_pairs={{0,2},{1,3},{2,0},{3,1},{4,6},{5,7},{6,4},{7,5},{8,10},{9,11},{10,... | collective-permute-start | bytes 786440 | tf_op jit(solution)/shard_map/ppermute | solution.py:363
  10.5 0.2 collective-permute-start.6
  10.7 0.0 slice-done
  10.7 1.0 %copy.8 = bf16[512,512]{0,1:T(8,128)(2,1)} copy(bf16[512,512]{1,0:T(8,128)(2,1)S(1)} %slice-done) | data formatting | bytes 1048576
  11.7 0.0 copy-done.6
  11.7 0.0 copy-start.2
  11.7 1.0 %copy-done.2 = bf16[512,512]{0,1:T(8,128)(2,1)S(1)} copy-done((bf16[512,512]{0,1:T(8,128)(2,1)S(1)}, bf16[512,512]{0,1:T(8,128)(2,1)}, u32[]{:S(2)}) %copy-start.2) | copy-done | bytes 524312
  12.8 0.0 copy-start.4
  12.8 1.4 %copy-done.4 = bf16[512,1536]{1,0:T(8,128)(2,1)S(1)} copy-done((bf16[512,1536]{1,0:T(8,128)(2,1)S(1)}, bf16[512,1536]{1,0:T(8,128)(2,1)}, u32[]{:S(2)}) %copy-start.4) | copy-done | bytes 1572888
  14.2 3.9 %attend_time.1.refs_1_ = bf16[2,16,4,8,512]{4,3,2,1,0:T(8,128)(2,1)S(1)} custom-call(f32[1,512]{1,0:T(1,128)S(1)} %bitcast.16, bf16[512,1536]{1,0:T(8,128)(2,1)S(1)} %copy-done.4, bf16[512,512]{1,0:T(8,128)(2,1)S(1)} %bitcast.12, bf16[2,16,4,8,512]{4,3,2,1,0:T(8,128)(2,1)S(1)} %copy-done), custom_call_target="tpu_custom_call" | custom-call | flops 5750001152 | bytes 18451000 | tf_op jit(solution)/shard_map/attend_time/pallas_call | solution.py:122
  18.1 2.6 %all-to-all-done.refs_0_ = bf16[8,4,4,8,512]{4,3,2,1,0:T(8,128)(2,1)S(1)} async-done(((bf16[8,4,4,8,512]{4,3,2,1,0:T(8,128)(2,1)}), bf16[8,4,4,8,512]{4,3,2,1,0:T(8,128)(2,1)S(1)}, u32[]{:S(2)}, u32[]{:S(2)}) %all-to-all-start) | async-done | bytes 1048608 | tf_op jit(solution)/shard_map/all_to_all | solution.py:382
  20.7 0.0 copy-start.3
  20.7 1.0 %copy-done.3 = bf16[512,512]{0,1:T(8,128)(2,1)S(1)} copy-done((bf16[512,512]{0,1:T(8,128)(2,1)S(1)}, bf16[512,512]{0,1:T(8,128)(2,1)}, u32[]{:S(2)}) %copy-start.3) | copy-done | bytes 524312
  21.8 0.0 copy-start.5
  21.8 1.4 %copy-done.5 = bf16[512,1536]{1,0:T(8,128)(2,1)S(1)} copy-done((bf16[512,1536]{1,0:T(8,128)(2,1)S(1)}, bf16[512,1536]{1,0:T(8,128)(2,1)}, u32[]{:S(2)}) %copy-start.5) | copy-done | bytes 1572888
  23.2 4.3 %attend_x.1 = (bf16[2,4,4,8,512]{4,3,2,1,0:T(8,128)(2,1)S(1)}, bf16[2,4,4,8,512]{4,3,2,1,0:T(8,128)(2,1)S(1)}, bf16[2,4,4,8,512]{4,3,2,1,0:T(8,128)(2,1)S(1)}, bf16[2,4,4,8,512]{4,3,2,1,0:T(8,128)(2,1)S(1)}) custom-call(f32[1,512]{1,0:T(1,128)S(1)} %bitcast.17, bf16[512,1536]{1,0:T(8,128)(2,1)S(1)} %copy-done.5, bf16[512,512]{1,0:T(8,128)(2,1)S(1)} %bitcast.13, ...), custom_call_target="tpu_custom_call" | custom-call | flops 5750001152 | bytes 18451000 | tf_op jit(solution)/shard_map/attend_x/pallas_call | solution.py:122
  27.5 0.6 collective-permute-start
  28.1 0.6 %collective-permute-start.1 = (bf16[2,4,4,8,512]{4,3,2,1,0:T(8,128)(2,1)S(1)}, bf16[2,4,4,8,512]{4,3,2,1,0:T(8,128)(2,1)S(1)}, u32[]{:S(2)}, u32[]{:S(2)}) collective-permute-start(bf16[2,4,4,8,512]{4,3,2,1,0:T(8,128)(2,1)S(1)} %get-tuple-element.23), channel_id=1, source_target_pairs={{0,16},{4,20},{8,24},{12,28},{16,0},{20,4},{24,8},{28,12},{1,17},{... | collective-permute-start | bytes 786440 | tf_op jit(solution)/shard_map/ppermute | solution.py:363
  28.7 0.0 collective-permute-done.4.refs_1_
  28.8 2.3 %collective-permute-start.2 = (bf16[2,4,4,8,512]{4,3,2,1,0:T(8,128)(2,1)S(1)}, bf16[2,4,4,8,512]{4,3,2,1,0:T(8,128)(2,1)S(1)}, u32[]{:S(2)}, u32[]{:S(2)}) collective-permute-start(bf16[2,4,4,8,512]{4,3,2,1,0:T(8,128)(2,1)S(1)} %get-tuple-element.24), channel_id=1, source_target_pairs={{0,24},{4,28},{8,16},{12,20},{16,8},{20,12},{24,0},{28,4},{1,25},{... | collective-permute-start | bytes 786440 | tf_op jit(solution)/shard_map/ppermute | solution.py:363
  31.1 0.0 collective-permute-done.5.refs_2_
  31.1 0.0 collective-permute-done.6.refs_3_
  31.1 3.5 %attend_y.2 = (bf16[4,4,8,512]{3,2,1,0:T(8,128)(2,1)S(1)}, bf16[4,4,8,512]{3,2,1,0:T(8,128)(2,1)S(1)}, bf16[4,4,8,512]{3,2,1,0:T(8,128)(2,1)S(1)}, bf16[4,4,8,512]{3,2,1,0:T(8,128)(2,1)S(1)}) custom-call(f32[1,512]{1,0:T(1,128)S(1)} %bitcast.18, bf16[512,1536]{1,0:T(8,128)(2,1)S(1)} %copy-done.5, bf16[512,512]{1,0:T(8,128)(2,1)S(1)} %bitcast.14, ...), custom_call_target="tpu_custom_call" | custom-call | flops 5750001152 | bytes 18451000 | tf_op jit(solution)/shard_map/attend_y/pallas_call | solution.py:122
  34.5 3.7 %collective-permute-start.10 = (bf16[4,4,8,512]{3,2,1,0:T(8,128)(2,1)S(1)}, bf16[4,4,8,512]{3,2,1,0:T(8,128)(2,1)S(1)}, u32[]{:S(2)}, u32[]{:S(2)}) collective-permute-start(bf16[4,4,8,512]{3,2,1,0:T(8,128)(2,1)S(1)} %get-tuple-element.34), channel_id=1, source_target_pairs={{0,3},{1,2},{2,1},{3,0},{4,7},{5,6},{6,5},{7,4},{8,11},{9,10},{10,... | collective-permute-start | bytes 393224 | tf_op jit(solution)/shard_map/ppermute | solution.py:363
  38.2 1.8 %collective-permute-start.11 = (bf16[4,4,8,512]{3,2,1,0:T(8,128)(2,1)S(1)}, bf16[4,4,8,512]{3,2,1,0:T(8,128)(2,1)S(1)}, u32[]{:S(2)}, u32[]{:S(2)}) collective-permute-start(bf16[4,4,8,512]{3,2,1,0:T(8,128)(2,1)S(1)} %get-tuple-element.35), channel_id=1, source_target_pairs={{0,2},{1,3},{2,0},{3,1},{4,6},{5,7},{6,4},{7,5},{8,10},{9,11},{10,... | collective-permute-start | bytes 393224 | tf_op jit(solution)/shard_map/ppermute | solution.py:363
  40.0 0.0 collective-permute-done.refs_1_
  40.0 0.1 collective-permute-start.12
  40.1 1.7 %collective-permute-done.1.refs_2_ = bf16[2,4,4,8,512]{4,3,2,1,0:T(8,128)(2,1)S(1)} collective-permute-done((bf16[2,4,4,8,512]{4,3,2,1,0:T(8,128)(2,1)S(1)}, bf16[2,4,4,8,512]{4,3,2,1,0:T(8,128)(2,1)S(1)}, u32[]{:S(2)}, u32[]{:S(2)}) %collective-permute-start.1) | collective-permute-done | bytes 262176 | tf_op jit(solution)/shard_map/ppermute | solution.py:363
  41.8 0.0 collective-permute-done.2.refs_3_
  41.8 0.9 %pack_x.1 = bf16[4,4,4,8,512]{4,3,2,1,0:T(8,128)(2,1)S(1)} custom-call(bf16[2,4,4,8,512]{4,3,2,1,0:T(8,128)(2,1)S(1)} %get-tuple-element.21.refs_0_.refs_4_, bf16[2,4,4,8,512]{4,3,2,1,0:T(8,128)(2,1)S(1)} %collective-permute-done.refs_1_, bf16[2,4,4,8,512]{4,3,2,1,0:T(8,128)(2,1)S(1)} %collective-permute-done.1.refs_2_, ...), custom_call_target="tpu_custom_call" | custom-call | flops 1000 | bytes 1000 | tf_op jit(solution)/shard_map/pack_x/pallas_call | solution.py:258
  42.7 0.1 collective-permute-start.3
  42.8 3.5 %attend_y.3 = (bf16[4,4,8,512]{3,2,1,0:T(8,128)(2,1)S(1)}, bf16[4,4,8,512]{3,2,1,0:T(8,128)(2,1)S(1)}, bf16[4,4,8,512]{3,2,1,0:T(8,128)(2,1)S(1)}, bf16[4,4,8,512]{3,2,1,0:T(8,128)(2,1)S(1)}) custom-call(f32[1,512]{1,0:T(1,128)S(1)} %bitcast.19, bf16[512,1536]{1,0:T(8,128)(2,1)S(1)} %copy-done.5, bf16[512,512]{1,0:T(8,128)(2,1)S(1)} %bitcast.15, ...), custom_call_target="tpu_custom_call" | custom-call | flops 5750001152 | bytes 18451000 | tf_op jit(solution)/shard_map/attend_y/pallas_call | solution.py:122
  46.3 1.6 %collective-permute-start.9 = (bf16[4,4,8,512]{3,2,1,0:T(8,128)(2,1)S(1)}, bf16[4,4,8,512]{3,2,1,0:T(8,128)(2,1)S(1)}, u32[]{:S(2)}, u32[]{:S(2)}) collective-permute-start(bf16[4,4,8,512]{3,2,1,0:T(8,128)(2,1)S(1)} %get-tuple-element.33), channel_id=1, source_target_pairs={{0,1},{1,0},{2,3},{3,2},{4,5},{5,4},{6,7},{7,6},{8,9},{9,8},{10,11... | collective-permute-start | bytes 393224 | tf_op jit(solution)/shard_map/ppermute | solution.py:363
  47.9 0.0 collective-permute-done.10.refs_1_
  47.9 2.6 %collective-permute-start.7 = (bf16[4,4,8,512]{3,2,1,0:T(8,128)(2,1)S(1)}, bf16[4,4,8,512]{3,2,1,0:T(8,128)(2,1)S(1)}, u32[]{:S(2)}, u32[]{:S(2)}) collective-permute-start(bf16[4,4,8,512]{3,2,1,0:T(8,128)(2,1)S(1)} %get-tuple-element.30), channel_id=1, source_target_pairs={{0,2},{1,3},{2,0},{3,1},{4,6},{5,7},{6,4},{7,5},{8,10},{9,11},{10,... | collective-permute-start | bytes 393224 | tf_op jit(solution)/shard_map/ppermute | solution.py:363
  50.5 0.0 collective-permute-done.3.refs_4_
  50.5 0.2 collective-permute-start.8
  50.7 0.0 copy-start.1
  50.7 0.2 add_x.1.base_ref
  51.0 0.0 collective-permute-done.11.refs_2_
  51.0 0.0 collective-permute-done.12.refs_3_
  51.0 0.8 %copy-done.1 = bf16[512,512]{1,0:T(8,128)(2,1)S(1)} copy-done((bf16[512,512]{1,0:T(8,128)(2,1)S(1)}, bf16[512,512]{1,0:T(8,128)(2,1)}, u32[]{:S(2)}) %copy-start.1) | copy-done | bytes 524312
  51.8 1.2 %finish.3.refs_2_ = bf16[32,4,8,512]{3,2,1,0:T(8,128)(2,1)} custom-call(bf16[512,512]{1,0:T(8,128)(2,1)S(1)} %copy-done.1, bf16[32,4,8,512]{3,2,1,0:T(8,128)(2,1)S(1)} %bitcast.8, f32[32,4,8,512]{3,2,1,0:T(8,128)S(1)} %add_x.1.base_ref, bf16[4,4,8,512]{3,2,1,0:T(8,128)(2,1)S(1)} %get-tuple-element.29.refs_4_.refs_0_, ...), custom_call_target="tpu_custom_call" | custom-call | flops 1000 | bytes 1000 | tf_op jit(solution)/shard_map/finish/pallas_call | solution.py:317
  52.9 2.1 %collective-permute-done.9.refs_1_ = bf16[4,4,8,512]{3,2,1,0:T(8,128)(2,1)S(1)} collective-permute-done((bf16[4,4,8,512]{3,2,1,0:T(8,128)(2,1)S(1)}, bf16[4,4,8,512]{3,2,1,0:T(8,128)(2,1)S(1)}, u32[]{:S(2)}, u32[]{:S(2)}) %collective-permute-start.9) | collective-permute-done | bytes 131104 | tf_op jit(solution)/shard_map/ppermute | solution.py:363
  55.0 1.0 %finish.4.refs_2_ = bf16[32,4,8,512]{3,2,1,0:T(8,128)(2,1)} custom-call(bf16[512,512]{1,0:T(8,128)(2,1)S(1)} %copy-done.1, bf16[32,4,8,512]{3,2,1,0:T(8,128)(2,1)S(1)} %bitcast.9, f32[32,4,8,512]{3,2,1,0:T(8,128)S(1)} %add_x.1.base_ref, bf16[4,4,8,512]{3,2,1,0:T(8,128)(2,1)S(1)} %get-tuple-element.32.refs_0_, ...), custom_call_target="tpu_custom_call", output_to_operand_aliasing={{}: (5, {})} | custom-call | flops 1000 | bytes 1000 | tf_op jit(solution)/shard_map/finish/pallas_call | solution.py:317
  56.0 4.8 %collective-permute-done.7.refs_0_ = bf16[4,4,8,512]{3,2,1,0:T(8,128)(2,1)S(1)} collective-permute-done((bf16[4,4,8,512]{3,2,1,0:T(8,128)(2,1)S(1)}, bf16[4,4,8,512]{3,2,1,0:T(8,128)(2,1)S(1)}, u32[]{:S(2)}, u32[]{:S(2)}) %collective-permute-start.7) | collective-permute-done | bytes 131104 | tf_op jit(solution)/shard_map/ppermute | solution.py:363
  60.8 0.0 collective-permute-done.8.refs_1_
  60.8 1.0 %finish.5 = bf16[32,4,8,512]{3,2,1,0:T(8,128)(2,1)} custom-call(bf16[512,512]{1,0:T(8,128)(2,1)S(1)} %copy-done.1, bf16[32,4,8,512]{3,2,1,0:T(8,128)(2,1)S(1)} %bitcast.10, f32[32,4,8,512]{3,2,1,0:T(8,128)S(1)} %add_x.1.base_ref, bf16[4,4,8,512]{3,2,1,0:T(8,128)(2,1)S(1)} %collective-permute-done.7.refs_0_, ...), custom_call_target="tpu_custom_call", output_to_operand_aliasing={{}: (5, {})} | custom-call | flops 1000 | bytes 1000 | tf_op jit(solution)/shard_map/finish/pallas_call | solution.py:317
Async XLA Ops:
  0.0 5.3 %copy-start = (bf16[2,16,4,8,512]{4,3,2,1,0:T(8,128)(2,1)S(1)}, bf16[2,16,4,8,512]{4,3,2,1,0:T(8,128)(2,1)}, u32[]{:S(2)}) copy-start(bf16[2,16,4,8,512]{4,3,2,1,0:T(8,128)(2,1)} %refs_0_.1) | copy-start | bytes 3145732
  0.0 10.7 %slice-start = ((bf16[512,1536]{1,0:T(8,128)(2,1)}), bf16[512,512]{1,0:T(8,128)(2,1)S(1)}, s32[]{:S(2)}) async-start(bf16[512,1536]{1,0:T(8,128)(2,1)} %w_ref.10), calls=%async_computation.1 | async-start | bytes 1048576 | tf_op jit(solution)/shard_map/slice | solution.py:376
  0.0 20.7 %all-to-all-start = ((bf16[8,4,4,8,512]{4,3,2,1,0:T(8,128)(2,1)}), bf16[8,4,4,8,512]{4,3,2,1,0:T(8,128)(2,1)S(1)}, u32[]{:S(2)}, u32[]{:S(2)}) async-start(bf16[8,4,4,8,512]{4,3,2,1,0:T(8,128)(2,1)} %bitcast.6), calls=%async_computation | async-start | bytes 2097152 | tf_op jit(solution)/shard_map/all_to_all | solution.py:382
  5.3 6.4 %copy-start.6 = (f32[512]{0:T(512)S(1)}, f32[512]{0:T(512)}, u32[]{:S(2)}) copy-start(f32[512]{0:T(512)} %param.5) | copy-start | bytes 6148
  6.3 22.5 %collective-permute-start.4 = (bf16[8,4,8,512]{3,2,1,0:T(8,128)(2,1)}, bf16[8,4,8,512]{3,2,1,0:T(8,128)(2,1)}, u32[]{:S(2)}, u32[]{:S(2)}) collective-permute-start(bf16[8,4,8,512]{3,2,1,0:T(8,128)(2,1)} %get-tuple-element.26), channel_id=1, source_target_pairs={{0,1},{1,0},{2,3},{3,2},{4,5},{5,4},{6,7},{7,6},{8,9},{9,8},{10,11... | collective-permute-start | bytes 786440 | tf_op jit(solution)/shard_map/ppermute | solution.py:363
  7.9 23.1 %collective-permute-start.5 = (bf16[8,4,8,512]{3,2,1,0:T(8,128)(2,1)}, bf16[8,4,8,512]{3,2,1,0:T(8,128)(2,1)}, u32[]{:S(2)}, u32[]{:S(2)}) collective-permute-start(bf16[8,4,8,512]{3,2,1,0:T(8,128)(2,1)} %get-tuple-element.27), channel_id=1, source_target_pairs={{0,2},{1,3},{2,0},{3,1},{4,6},{5,7},{6,4},{7,5},{8,10},{9,11},{10,... | collective-permute-start | bytes 786440 | tf_op jit(solution)/shard_map/ppermute | solution.py:363
  10.5 20.6 %collective-permute-start.6 = (bf16[8,4,8,512]{3,2,1,0:T(8,128)(2,1)}, bf16[8,4,8,512]{3,2,1,0:T(8,128)(2,1)}, u32[]{:S(2)}, u32[]{:S(2)}) collective-permute-start(bf16[8,4,8,512]{3,2,1,0:T(8,128)(2,1)} %get-tuple-element.28), channel_id=1, source_target_pairs={{0,3},{1,2},{2,1},{3,0},{4,7},{5,6},{6,5},{7,4},{8,11},{9,10},{10,... | collective-permute-start | bytes 786440 | tf_op jit(solution)/shard_map/ppermute | solution.py:363
  11.7 1.0 %copy-start.2 = (bf16[512,512]{0,1:T(8,128)(2,1)S(1)}, bf16[512,512]{0,1:T(8,128)(2,1)}, u32[]{:S(2)}) copy-start(bf16[512,512]{0,1:T(8,128)(2,1)} %copy.8) | copy-start | bytes 1572868
  12.8 1.4 %copy-start.4 = (bf16[512,1536]{1,0:T(8,128)(2,1)S(1)}, bf16[512,1536]{1,0:T(8,128)(2,1)}, u32[]{:S(2)}) copy-start(bf16[512,1536]{1,0:T(8,128)(2,1)} %w_ref.10) | copy-start | bytes 4718596
  20.7 1.0 %copy-start.3 = (bf16[512,512]{0,1:T(8,128)(2,1)S(1)}, bf16[512,512]{0,1:T(8,128)(2,1)}, u32[]{:S(2)}) copy-start(bf16[512,512]{0,1:T(8,128)(2,1)} %copy.8) | copy-start | bytes 1572868
  21.8 1.4 %copy-start.5 = (bf16[512,1536]{1,0:T(8,128)(2,1)S(1)}, bf16[512,1536]{1,0:T(8,128)(2,1)}, u32[]{:S(2)}) copy-start(bf16[512,1536]{1,0:T(8,128)(2,1)} %w_ref.10) | copy-start | bytes 4718596
  27.5 12.5 %collective-permute-start = (bf16[2,4,4,8,512]{4,3,2,1,0:T(8,128)(2,1)S(1)}, bf16[2,4,4,8,512]{4,3,2,1,0:T(8,128)(2,1)S(1)}, u32[]{:S(2)}, u32[]{:S(2)}) collective-permute-start(bf16[2,4,4,8,512]{4,3,2,1,0:T(8,128)(2,1)S(1)} %get-tuple-element.22), channel_id=1, source_target_pairs={{0,8},{4,12},{8,0},{12,4},{16,24},{20,28},{24,16},{28,20},{1,9},{5... | collective-permute-start | bytes 786440 | tf_op jit(solution)/shard_map/ppermute | solution.py:363
  28.1 13.7 %collective-permute-start.1 = (bf16[2,4,4,8,512]{4,3,2,1,0:T(8,128)(2,1)S(1)}, bf16[2,4,4,8,512]{4,3,2,1,0:T(8,128)(2,1)S(1)}, u32[]{:S(2)}, u32[]{:S(2)}) collective-permute-start(bf16[2,4,4,8,512]{4,3,2,1,0:T(8,128)(2,1)S(1)} %get-tuple-element.23), channel_id=1, source_target_pairs={{0,16},{4,20},{8,24},{12,28},{16,0},{20,4},{24,8},{28,12},{1,17},{... | collective-permute-start | bytes 786440 | tf_op jit(solution)/shard_map/ppermute | solution.py:363
  28.8 13.1 %collective-permute-start.2 = (bf16[2,4,4,8,512]{4,3,2,1,0:T(8,128)(2,1)S(1)}, bf16[2,4,4,8,512]{4,3,2,1,0:T(8,128)(2,1)S(1)}, u32[]{:S(2)}, u32[]{:S(2)}) collective-permute-start(bf16[2,4,4,8,512]{4,3,2,1,0:T(8,128)(2,1)S(1)} %get-tuple-element.24), channel_id=1, source_target_pairs={{0,24},{4,28},{8,16},{12,20},{16,8},{20,12},{24,0},{28,4},{1,25},{... | collective-permute-start | bytes 786440 | tf_op jit(solution)/shard_map/ppermute | solution.py:363
  34.5 13.4 %collective-permute-start.10 = (bf16[4,4,8,512]{3,2,1,0:T(8,128)(2,1)S(1)}, bf16[4,4,8,512]{3,2,1,0:T(8,128)(2,1)S(1)}, u32[]{:S(2)}, u32[]{:S(2)}) collective-permute-start(bf16[4,4,8,512]{3,2,1,0:T(8,128)(2,1)S(1)} %get-tuple-element.34), channel_id=1, source_target_pairs={{0,3},{1,2},{2,1},{3,0},{4,7},{5,6},{6,5},{7,4},{8,11},{9,10},{10,... | collective-permute-start | bytes 393224 | tf_op jit(solution)/shard_map/ppermute | solution.py:363
  38.2 12.8 %collective-permute-start.11 = (bf16[4,4,8,512]{3,2,1,0:T(8,128)(2,1)S(1)}, bf16[4,4,8,512]{3,2,1,0:T(8,128)(2,1)S(1)}, u32[]{:S(2)}, u32[]{:S(2)}) collective-permute-start(bf16[4,4,8,512]{3,2,1,0:T(8,128)(2,1)S(1)} %get-tuple-element.35), channel_id=1, source_target_pairs={{0,2},{1,3},{2,0},{3,1},{4,6},{5,7},{6,4},{7,5},{8,10},{9,11},{10,... | collective-permute-start | bytes 393224 | tf_op jit(solution)/shard_map/ppermute | solution.py:363
  40.0 11.0 %collective-permute-start.12 = (bf16[4,4,8,512]{3,2,1,0:T(8,128)(2,1)S(1)}, bf16[4,4,8,512]{3,2,1,0:T(8,128)(2,1)S(1)}, u32[]{:S(2)}, u32[]{:S(2)}) collective-permute-start(bf16[4,4,8,512]{3,2,1,0:T(8,128)(2,1)S(1)} %get-tuple-element.36), channel_id=1, source_target_pairs={{0,1},{1,0},{2,3},{3,2},{4,5},{5,4},{6,7},{7,6},{8,9},{9,8},{10,11... | collective-permute-start | bytes 393224 | tf_op jit(solution)/shard_map/ppermute | solution.py:363
  42.7 7.8 %collective-permute-start.3 = (bf16[4,4,4,8,512]{4,3,2,1,0:T(8,128)(2,1)S(1)}, bf16[4,4,4,8,512]{4,3,2,1,0:T(8,128)(2,1)S(1)}, u32[]{:S(2)}, u32[]{:S(2)}) collective-permute-start(bf16[4,4,4,8,512]{4,3,2,1,0:T(8,128)(2,1)S(1)} %pack_x.1), channel_id=1, source_target_pairs={{0,4},{4,0},{8,12},{12,8},{16,20},{20,16},{24,28},{28,24},{1,5},{5... | collective-permute-start | bytes 1572872 | tf_op jit(solution)/shard_map/ppermute | solution.py:395
  46.3 8.7 %collective-permute-start.9 = (bf16[4,4,8,512]{3,2,1,0:T(8,128)(2,1)S(1)}, bf16[4,4,8,512]{3,2,1,0:T(8,128)(2,1)S(1)}, u32[]{:S(2)}, u32[]{:S(2)}) collective-permute-start(bf16[4,4,8,512]{3,2,1,0:T(8,128)(2,1)S(1)} %get-tuple-element.33), channel_id=1, source_target_pairs={{0,1},{1,0},{2,3},{3,2},{4,5},{5,4},{6,7},{7,6},{8,9},{9,8},{10,11... | collective-permute-start | bytes 393224 | tf_op jit(solution)/shard_map/ppermute | solution.py:363
  47.9 12.9 %collective-permute-start.7 = (bf16[4,4,8,512]{3,2,1,0:T(8,128)(2,1)S(1)}, bf16[4,4,8,512]{3,2,1,0:T(8,128)(2,1)S(1)}, u32[]{:S(2)}, u32[]{:S(2)}) collective-permute-start(bf16[4,4,8,512]{3,2,1,0:T(8,128)(2,1)S(1)} %get-tuple-element.30), channel_id=1, source_target_pairs={{0,2},{1,3},{2,0},{3,1},{4,6},{5,7},{6,4},{7,5},{8,10},{9,11},{10,... | collective-permute-start | bytes 393224 | tf_op jit(solution)/shard_map/ppermute | solution.py:363
  50.5 10.3 %collective-permute-start.8 = (bf16[4,4,8,512]{3,2,1,0:T(8,128)(2,1)S(1)}, bf16[4,4,8,512]{3,2,1,0:T(8,128)(2,1)S(1)}, u32[]{:S(2)}, u32[]{:S(2)}) collective-permute-start(bf16[4,4,8,512]{3,2,1,0:T(8,128)(2,1)S(1)} %get-tuple-element.31), channel_id=1, source_target_pairs={{0,3},{1,2},{2,1},{3,0},{4,7},{5,6},{6,5},{7,4},{8,11},{9,10},{10,... | collective-permute-start | bytes 393224 | tf_op jit(solution)/shard_map/ppermute | solution.py:363
  50.7 1.0 %copy-start.1 = (bf16[512,512]{1,0:T(8,128)(2,1)S(1)}, bf16[512,512]{1,0:T(8,128)(2,1)}, u32[]{:S(2)}) copy-start(bf16[512,512]{1,0:T(8,128)(2,1)} %w_ref.13) | copy-start | bytes 1572868
